TPU v7x, 256 devices: a whole 4x4x8 slice. The times are simulated.
256 devices in a mesh: lat: 4 (over x_lo, core), lon: 64 (over z, y, x_hi).
Axes of the slice: x: 4 (x_hi: 2, x_lo: 2; x = x_hi * 2 + x_lo), y: 4, z: 8, core: 2. Of those that a mesh axis runs over, the one named last changes fastest.
Arguments:
- tokens: bfloat16 [64, 1024, 1536], P('lat', 'lon'), may hold values from -6 to 6
- cotangent: bfloat16 [64, 1024, 1536], P('lat', 'lon'), may hold values from -6 to 6
- gain: float32 [1536], replicated, may hold values from 0.5 to 1.5
- w_qkv: bfloat16 [1536, 4608], P('lon'), may hold values from -0.15625 to 0.15625
- w_out: bfloat16 [1536, 1536], P('lon'), may hold values from -0.15625 to 0.15625
- logit_scale: float32 [24], replicated, may hold values from 2 to 12
- region_ids: int32 [64, 1024], P('lat', 'lon'), may hold values from 0 to 2
Outputs:
- output: bfloat16 [64, 1024, 1536], P('lat', 'lon')
- grad_input: bfloat16 [64, 1024, 1536], P('lat', 'lon')
All inputs are finite; a program needn't handle non-finite values.
Results may differ from a plain program's by a relative error of at most 0.0071.
Values may be sent and summed in bfloat16 or wider, within the bound.
No kernel may reach another device: no remote copies, remote signals or barrier semaphores. Data moves between devices by JAX's collectives and lax.ppermute only.
A program may use at most 128 MiB of HBM per device.

v0:
```python
import functools
import itertools

import jax
import jax.numpy as jnp
from jax import lax
from jax.experimental import pallas as pl
from jax.experimental.pallas import tpu as pltpu
from jax.sharding import Mesh
from jax.sharding import PartitionSpec as P

SHIFT_LAT = 2
SHIFT_LON = 8
D = 1536
SIZES = {"xl": 2, "core": 2, "z": 8, "y": 4, "xh": 2}
AXES = tuple(SIZES)
LAT = ("xl", "core")
LON = ("z", "y", "xh")
TOK = 256
WIN = 64
PAIRS = 12
Y_ORDER = (0, 1, -1, 2)
UNITS = 32
UROWS = 48


def linear(place, axes):
    total = 0
    for axis in axes:
        total = total * SIZES[axis] + place[axis]
    return total


def permutation(target):
    pairs = []
    for values in itertools.product(*[range(SIZES[axis]) for axis in AXES]):
        place = dict(zip(AXES, values))
        goal = target(dict(place))
        if goal is not None:
            pairs.append((linear(place, AXES), linear(goal, AXES)))
    return pairs


def along(axis, step):
    def target(place):
        place[axis] = (place[axis] + step) % SIZES[axis]
        return place

    return permutation(target)


def across_x():
    def target(place):
        x = 3 - (place["xh"] * 2 + place["xl"])
        place["xh"], place["xl"] = x // 2, x % 2
        return place

    return permutation(target)


def send(value, pairs):
    return lax.ppermute(value, AXES, pairs)


def lon_ring(value, step):
    size = SIZES["z"] * SIZES["y"] * SIZES["xh"]
    return lax.ppermute(value, LON, [(i, (i + step) % size) for i in range(size)])


def lat_line(value, step):
    size = SIZES["xl"] * SIZES["core"]
    return lax.ppermute(
        value, LAT, [(i, i + step) for i in range(size) if 0 <= i + step < size]
    )


def after(value, *others):
    return lax.optimization_barrier((value,) + others)[0]


def ring_step(ahead, behind, axis):
    return send(ahead, along(axis, 1)), send(behind, along(axis, -1))


def gather_weights(w_qkv, w_out):
    core = lax.axis_index("core")
    x_hi = lax.axis_index("xh")
    first = jnp.where(core == 0, w_qkv[:, :D], w_qkv[:, 2 * D :])
    second = jnp.where(core == 0, w_qkv[:, D : 2 * D], w_out)

    def cross(block):
        other = send(block, across_x())
        low = jnp.where(x_hi == 0, block, other)
        high = jnp.where(x_hi == 0, other, block)
        return jnp.concatenate([low, high])[None]

    def far_ring(block, axis, reach):
        up = down = block
        got = [(0, 0, block)]
        for step in range(1, reach):
            up, down = ring_step(up, down, axis)
            got += [(step, 0, up), (-step, 0, down)]
        got.append((reach, 0, send(up[..., : D // 2], along(axis, 1))))
        got.append((-reach, D // 2, send(down[..., D // 2 :], along(axis, -1))))
        return got

    first, second = cross(first), cross(second)
    first = jnp.concatenate([first] + [send(first, along("y", s)) for s in Y_ORDER[1:]])
    up = down = second
    parts = [second]
    for _ in range(1, 4):
        up, down = ring_step(up, down, "z")
        parts += [up, down]
    parts.append(send(up, along("z", 1)))
    second = jnp.concatenate(parts)
    zs = (0, 1, -1, 2, -2, 3, -3, 4)
    found = [([(d, s) for s in Y_ORDER], c, b) for d, c, b in far_ring(first, "z", 4)]
    early = found[1][2]
    found += [([(s, d) for s in zs], D + c, b) for d, c, b in far_ring(second, "y", 2)]
    plan, blocks = [], []
    for distances, column, block in found:
        plan += [(tuple(distances), column, 0), (tuple(distances), column, 1)]
        blocks += [block, send(block, along("core", 1))]
    return plan, blocks, early


def pull_ahead(tensor, early):
    edge = lon_ring(after(tensor[:, :, :SHIFT_LON], early), -1)
    widened = jnp.concatenate([tensor[:, :, SHIFT_LON:], edge], axis=2)
    rim = lat_line(widened[:, :SHIFT_LAT], -1)
    return jnp.concatenate([widened[:, SHIFT_LAT:], rim], axis=1)


def pull_behind(tensor):
    lats, lons = SIZES["xl"] * SIZES["core"], SIZES["z"] * SIZES["y"] * SIZES["xh"]
    diagonal = [
        (a * lons + b, (a + 1) * lons + (b + 1) % lons) for a in range(lats - 1) for b in range(lons)
    ]
    edge = lon_ring(tensor[:, :-SHIFT_LAT, -SHIFT_LON:], 1)
    rim = lat_line(tensor[:, -SHIFT_LAT:, :-SHIFT_LON], 1)
    corner = send(tensor[:, -SHIFT_LAT:, -SHIFT_LON:], diagonal)
    upper = jnp.concatenate([corner, rim], axis=2)
    lower = jnp.concatenate([edge, tensor[:, :-SHIFT_LAT, :-SHIFT_LON]], axis=2)
    return jnp.concatenate([upper, lower], axis=1)


def mm(a, b):
    return lax.dot_general(a, b, (((1,), (0,)), ((), ())), preferred_element_type=jnp.float32)


def mm_nt(a, b):
    return lax.dot_general(a, b, (((1,), (1,)), ((), ())), preferred_element_type=jnp.float32)


def mm_tn(a, b):
    return lax.dot_general(a, b, (((0,), (0,)), ((), ())), preferred_element_type=jnp.float32)


def bf(value):
    return value.astype(jnp.bfloat16)


def sum_heads(value, ones):
    high = bf(value)
    low = bf(value - high.astype(jnp.float32))
    return mm(jnp.concatenate([high, low], axis=1), ones)


def window_kernel(plan, pos, xs, gs, mask, gain, scale, *refs):
    count = len(plan)
    blocks = refs[:count]
    result, weights, normed, gatt, packed, attended, sem = refs[count:]
    z, y, core = pos[0], pos[1], pos[2]

    for (distances, column, sibling), block in zip(plan, blocks):
        side = lax.rem(core + sibling, 2)
        cols = pl.ds(column, block.shape[2])
        for j, (dz, dy) in enumerate(distances):
            unit = lax.rem(z - dz + 8, 8) * 4 + lax.rem(y - dy + 4, 4)
            pltpu.make_async_copy(block.at[j], weights.at[side, unit, :, cols], sem.at[side]).start()

    for i in range(4):
        rows = pl.ds(i * WIN, WIN)
        x = xs[rows, :].astype(jnp.float32)
        centre = x - jnp.mean(x, axis=-1, keepdims=True)
        spread = jnp.mean(centre * centre, axis=-1, keepdims=True)
        normed[rows, :] = bf(centre * lax.rsqrt(spread + 1e-05) * gain[...])

    for side in (1, 0):
        pltpu.make_async_copy(weights.at[side], weights.at[side], sem.at[side]).wait()

    @pl.loop(0, 2)
    def _(i):
        w = weights[1, pl.ds(i * 16, 16), :, D:].reshape(768, D)
        gatt[:, pl.ds(pl.multiple_of(i * 768, 128), 768)] = bf(mm_nt(gs[...], w))

    for m in range(3):

        @pl.loop(0, 3)
        def _(i, m=m):
            start = (m % 2) * D
            w = weights[m // 2, :, :, pl.ds(pl.multiple_of(start + i * 512, 128), 512)].reshape(D, 512)
            packed[:, pl.ds(pl.multiple_of(m * D + i * 512, 128), 512)] = bf(mm(normed[...], w))

    lane = lax.broadcasted_iota(jnp.int32, (256, 128), 1)
    row = lax.broadcasted_iota(jnp.int32, (256, 128), 0)
    same = (lane < 64) == (lax.rem(row, 128) < 64)
    ones = jnp.where(same, 1.0, 0.0).astype(jnp.bfloat16)
    left = lax.broadcasted_iota(jnp.int32, (WIN, 128), 1) < 64
    windows = [slice(i * WIN, (i + 1) * WIN) for i in range(4)]

    def spread_heads(block):
        zero = jnp.zeros_like(block)
        return jnp.concatenate([jnp.where(left, block, zero), jnp.where(left, zero, block)], axis=0)

    def fold_heads(block):
        return jnp.where(left, block[:WIN], block[WIN:])

    def each(function, *values):
        return jnp.concatenate([function(*[v[i] if isinstance(v, list) else v[part] for v in values]) for i, part in enumerate(windows)])

    @pl.loop(0, PAIRS)
    def _(p):
        at_q = pl.ds(pl.multiple_of(p * 128, 128), 128)
        at_k = pl.ds(pl.multiple_of(D + p * 128, 128), 128)
        at_v = pl.ds(pl.multiple_of(2 * D + p * 128, 128), 128)
        q = packed[:, at_q].astype(jnp.float32)
        k = packed[:, at_k].astype(jnp.float32)
        v = packed[:, at_v]
        d_out = gatt[:, at_q]
        factor = scale[pl.ds(p, 1), :]
        rq = lax.rsqrt(sum_heads(q * q, ones) + 1e-06)
        rk = lax.rsqrt(sum_heads(k * k, ones) + 1e-06)
        qn, kn = q * rq, k * rk
        qb, kb = bf(qn), bf(kn)
        k2 = [spread_heads(kb[part]) for part in windows]
        v2 = [spread_heads(v[part]) for part in windows]
        score = each(mm_nt, qb, k2)
        d_prob = each(mm_nt, d_out, v2)
        weight = jnp.exp(score * factor) * mask[...]
        prob = weight / sum_heads(weight, ones)
        prob16 = bf(prob)
        d_score = bf(prob * (d_prob - sum_heads(prob * d_prob, ones)) * factor)
        out = each(mm, prob16, v2)
        dv = each(lambda a, b: fold_heads(mm_tn(a, b)), prob16, d_out)
        dq = each(mm, d_score, k2)
        dk = each(lambda a, b: fold_heads(mm_tn(a, b)), d_score, qb)
        dq = rq * (dq - qn * sum_heads(qn * dq, ones))
        dk = rk * (dk - kn * sum_heads(kn * dk, ones))
        attended[:, at_q] = bf(out)
        packed[:, at_q] = bf(dq)
        packed[:, at_k] = bf(dk)
        packed[:, at_v] = bf(dv)

    @pl.loop(0, 3)
    def _(i):
        at = pl.ds(pl.multiple_of(i * 512, 128), 512)
        w = weights[1, :, :, pl.ds(pl.multiple_of(D + i * 512, 128), 512)].reshape(D, 512)
        result[0, :, at] = bf(mm(attended[...], w))

    @pl.loop(0, 2)
    def _(i):
        unit = pl.ds(i * 16, 16)
        total = mm_nt(packed[:, : 2 * D], weights[0, unit].reshape(768, 2 * D))
        total += mm_nt(packed[:, 2 * D :], weights[1, unit, :, :D].reshape(768, D))
        result[1, :, pl.ds(pl.multiple_of(i * 768, 128), 768)] = bf(total)


def window_attention(pos, xs, gs, mask, gain, scale, plan, blocks):
    vmem = pl.BlockSpec(memory_space=pltpu.VMEM)
    return pl.pallas_call(
        functools.partial(window_kernel, plan),
        out_shape=jax.ShapeDtypeStruct((2, TOK, D), jnp.bfloat16),
        in_specs=[pl.BlockSpec(memory_space=pltpu.SMEM)]
        + [vmem] * 5
        + [pl.BlockSpec(memory_space=pl.ANY)] * len(blocks),
        out_specs=vmem,
        scratch_shapes=[
            pltpu.VMEM((2, UNITS, UROWS, 2 * D), jnp.bfloat16),
            pltpu.VMEM((TOK, D), jnp.bfloat16),
            pltpu.VMEM((TOK, D), jnp.bfloat16),
            pltpu.VMEM((TOK, 3 * D), jnp.bfloat16),
            pltpu.VMEM((TOK, D), jnp.bfloat16),
            pltpu.SemaphoreType.DMA((2,)),
        ],
        compiler_params=pltpu.CompilerParams(vmem_limit_bytes=56 * 1024 * 1024),
        cost_estimate=pl.CostEstimate(
            flops=11 * 10**9, bytes_accessed=24 * 10**6, transcendentals=2 * 10**6
        ),
        name="window_attention",
    )(pos, xs, gs, mask, gain, scale, *blocks)


def finish_kernel(tokens, cotangent, moved, gain, out, grad_in):
    for i in range(4):
        rows = pl.ds(i * WIN, WIN)
        x = tokens[rows, :].astype(jnp.float32)
        out[rows, :] = bf(x + moved[0, rows, :].astype(jnp.float32))
        centre = x - jnp.mean(x, axis=-1, keepdims=True)
        r = lax.rsqrt(jnp.mean(centre * centre, axis=-1, keepdims=True) + 1e-05)
        unit = centre * r
        g = moved[1, rows, :].astype(jnp.float32) * gain[...]
        pull = g - jnp.mean(g, axis=-1, keepdims=True)
        pull -= unit * jnp.mean(g * unit, axis=-1, keepdims=True)
        grad_in[rows, :] = bf(pull * r + cotangent[rows, :].astype(jnp.float32))


def finish(tokens, cotangent, moved, gain):
    vmem = pl.BlockSpec(memory_space=pltpu.VMEM)
    return pl.pallas_call(
        finish_kernel,
        out_shape=[jax.ShapeDtypeStruct((TOK, D), jnp.bfloat16)] * 2,
        in_specs=[vmem] * 4,
        out_specs=[vmem, vmem],
        compiler_params=pltpu.CompilerParams(vmem_limit_bytes=32 * 1024 * 1024),
        name="finish",
    )(tokens, cotangent, moved, gain)


def body(tokens, cotangent, gain, w_qkv, w_out, logit_scale, region_ids):
    lat, lon, _ = tokens.shape
    plan, blocks, early = gather_weights(w_qkv, w_out)
    shifted = pull_ahead(jnp.stack([tokens, cotangent]), early)
    shifted = shifted.reshape(2, TOK, D)
    gain = gain[None]
    scale = jnp.repeat(logit_scale, 64).reshape(PAIRS, 128)
    region = region_ids.reshape(4, WIN)
    row = lax.axis_index(LAT) * lat + lax.broadcasted_iota(jnp.int32, (lat, lon), 0)
    total_lat = lat * SIZES["xl"] * SIZES["core"]
    valid = (row + SHIFT_LAT < total_lat).reshape(4, WIN)
    allowed = (region[:, :, None] == region[:, None, :]) & (
        valid[:, None, :] | jnp.eye(WIN, dtype=bool)[None]
    )
    mask = allowed.astype(jnp.float32).reshape(TOK, WIN)
    mask = jnp.concatenate([mask, mask], axis=1)
    pos = jnp.stack([lax.axis_index("z"), lax.axis_index("y"), lax.axis_index("core")]).astype(jnp.int32)
    moved = window_attention(pos, shifted[0], shifted[1], mask, gain, scale, plan, blocks)
    moved = pull_behind(moved.reshape(2, lat, lon, D)).reshape(2, TOK, D)
    output, grad_input = finish(
        tokens.reshape(TOK, D), cotangent.reshape(TOK, D), moved, gain
    )
    return output.reshape(lat, lon, D), grad_input.reshape(lat, lon, D)


def solution(mesh):
    fine = Mesh(mesh.devices.reshape(tuple(SIZES.values())), AXES)
    grid = P(LAT, LON, None)
    return jax.shard_map(
        body,
        mesh=fine,
        in_specs=(grid, grid, P(), P(LON, None), P(LON, None), P(), P(LAT, LON)),
        out_specs=(grid, grid),
        check_vma=False,
    )
```

profile of v0, /device:TPU:1, one launch (start us, length us, event | category | flops | bytes accessed | tf_op | source)
XLA Modules:
  0.0 187.7 jit_solution(2646594305111612169)
XLA Ops:
  1.7 3.4 %collective-permute-start.23 = (bf16[24,1536]{1,0:T(8,128)(2,1)S(1)}, bf16[24,1536]{1,0:T(8,128)(2,1)S(1)}, u32[]{:S(2)}, u32[]{:S(2)}) collective-permute-start(bf16[24,1536]{1,0:T(8,128)(2,1)S(1)} %get-tuple-element.16), channel_id=1, source_target_pairs={{0,129},{1,128},{2,131},{3,130},{4,133},{5,132},{6,135},{7,134},{8... | collective-permute-start | bytes 221192 | tf_op jit(solution)/shard_map/ppermute | solution.py:62
  6.8 1.9 %collective-permute-start.24 = (bf16[1,48,1536]{2,1,0:T(8,128)(2,1)S(1)}, bf16[1,48,1536]{2,1,0:T(8,128)(2,1)S(1)}, u32[]{:S(2)}, u32[]{:S(2)}) collective-permute-start(bf16[1,48,1536]{2,1,0:T(8,128)(2,1)S(1)} %maximum_bitcast_fusion.1), channel_id=1, source_target_pairs={{0,8},{1,9},{2,10},{3,11},{4,12},{5,13},{6,14},{7,15},{8,16},{9,17... | collective-permute-start | bytes 442376 | tf_op jit(solution)/shard_map/ppermute | solution.py:62
  8.7 4.0 %collective-permute-start.25 = (bf16[1,48,1536]{2,1,0:T(8,128)(2,1)S(1)}, bf16[1,48,1536]{2,1,0:T(8,128)(2,1)S(1)}, u32[]{:S(2)}, u32[]{:S(2)}) collective-permute-start(bf16[1,48,1536]{2,1,0:T(8,128)(2,1)S(1)} %maximum_bitcast_fusion.1), channel_id=1, source_target_pairs={{0,56},{1,57},{2,58},{3,59},{4,60},{5,61},{6,62},{7,63},{8,0},{9,1... | collective-permute-start | bytes 442376 | tf_op jit(solution)/shard_map/ppermute | solution.py:62
  14.2 1.5 collective-permute-start.2
  15.7 1.6 collective-permute-start.3
  18.2 4.0 %collective-permute-done.3 = bf16[1,48,1536]{2,1,0:T(8,128)(2,1)S(1)} collective-permute-done((bf16[1,48,1536]{2,1,0:T(8,128)(2,1)S(1)}, bf16[1,48,1536]{2,1,0:T(8,128)(2,1)S(1)}, u32[]{:S(2)}, u32[]{:S(2)}) %collective-permute-start.3) | collective-permute-done | bytes 147488 | tf_op jit(solution)/shard_map/ppermute | solution.py:62
  22.4 2.7 %collective-permute-start.9 = (bf16[4,48,1536]{2,1,0:T(8,128)(2,1)S(1)}, bf16[4,48,1536]{2,1,0:T(8,128)(2,1)S(1)}, u32[]{:S(2)}, u32[]{:S(2)}) collective-permute-start(bf16[4,48,1536]{2,1,0:T(8,128)(2,1)S(1)} %pad_maximum_fusion.2.refs_0_), channel_id=1, source_target_pairs={{0,56},{1,57},{2,58},{3,59},{4,60},{5,61},{6,62},{7,63},{8,0},{9,1... | collective-permute-start | bytes 1769480 | tf_op jit(solution)/shard_map/ppermute | solution.py:62
  25.0 3.4 %collective-permute-start.7 = (bf16[4,48,1536]{2,1,0:T(8,128)(2,1)S(1)}, bf16[4,48,1536]{2,1,0:T(8,128)(2,1)S(1)}, u32[]{:S(2)}, u32[]{:S(2)}) collective-permute-start(bf16[4,48,1536]{2,1,0:T(8,128)(2,1)S(1)} %pad_maximum_fusion.2.refs_0_), channel_id=1, source_target_pairs={{0,64},{1,65},{2,66},{3,67},{4,68},{5,69},{6,70},{7,71},{8,72},{9,... | collective-permute-start | bytes 1769480 | tf_op jit(solution)/shard_map/ppermute | solution.py:62
  28.5 2.7 %collective-permute-start.27 = (bf16[1,48,1536]{2,1,0:T(8,128)(2,1)S(1)}, bf16[1,48,1536]{2,1,0:T(8,128)(2,1)S(1)}, u32[]{:S(2)}, u32[]{:S(2)}) collective-permute-start(bf16[1,48,1536]{2,1,0:T(8,128)(2,1)S(1)} %collective-permute-done.25), channel_id=1, source_target_pairs={{0,56},{1,57},{2,58},{3,59},{4,60},{5,61},{6,62},{7,63},{8,0},{9,1... | collective-permute-start | bytes 442376 | tf_op jit(solution)/shard_map/ppermute | solution.py:62
  31.3 7.4 %collective-permute-done.26 = bf16[1,48,1536]{2,1,0:T(8,128)(2,1)S(1)} collective-permute-done((bf16[1,48,1536]{2,1,0:T(8,128)(2,1)S(1)}, bf16[1,48,1536]{2,1,0:T(8,128)(2,1)S(1)}, u32[]{:S(2)}, u32[]{:S(2)}) %collective-permute-start.26) | collective-permute-done | bytes 147488 | tf_op jit(solution)/shard_map/ppermute | solution.py:62
  38.7 2.7 %collective-permute-start.29 = (bf16[1,48,1536]{2,1,0:T(8,128)(2,1)S(1)}, bf16[1,48,1536]{2,1,0:T(8,128)(2,1)S(1)}, u32[]{:S(2)}, u32[]{:S(2)}) collective-permute-start(bf16[1,48,1536]{2,1,0:T(8,128)(2,1)S(1)} %collective-permute-done.27), channel_id=1, source_target_pairs={{0,56},{1,57},{2,58},{3,59},{4,60},{5,61},{6,62},{7,63},{8,0},{9,1... | collective-permute-start | bytes 442376 | tf_op jit(solution)/shard_map/ppermute | solution.py:62
  41.4 2.5 %collective-permute-done.28 = bf16[1,48,1536]{2,1,0:T(8,128)(2,1)S(1)} collective-permute-done((bf16[1,48,1536]{2,1,0:T(8,128)(2,1)S(1)}, bf16[1,48,1536]{2,1,0:T(8,128)(2,1)S(1)}, u32[]{:S(2)}, u32[]{:S(2)}) %collective-permute-start.28) | collective-permute-done | bytes 147488 | tf_op jit(solution)/shard_map/ppermute | solution.py:62
  44.0 4.0 %collective-permute-start.5 = (bf16[2,16,8,1536]{3,2,1,0:T(8,128)(2,1)S(1)}, bf16[2,16,8,1536]{3,2,1,0:T(8,128)(2,1)S(1)}, u32[]{:S(2)}, u32[]{:S(2)}) collective-permute-start(bf16[2,16,8,1536]{3,2,1,0:T(8,128)(2,1)S(1)} %get-tuple-element.5), channel_id=1, source_target_pairs={{0,63},{1,0},{2,1},{3,2},{4,3},{5,4},{6,5},{7,6},{8,7},{9,8},{10,9... | collective-permute-start | bytes 2359304 | tf_op jit(solution)/shard_map/ppermute | solution.py:67
  49.9 2.6 %collective-permute-start.34 = (bf16[8,48,1536]{2,1,0:T(8,128)(2,1)S(1)}, bf16[8,48,1536]{2,1,0:T(8,128)(2,1)S(1)}, u32[]{:S(2)}, u32[]{:S(2)}) collective-permute-start(bf16[8,48,1536]{2,1,0:T(8,128)(2,1)S(1)} %constant_dynamic-update-slice_fusion.refs_18_), channel_id=1, source_target_pairs={{0,6},{1,7},{2,0},{3,1},{4,2},{5,3},{6,4},{7,5},{8,14},{9,15},{10,... | collective-permute-start | bytes 3538952 | tf_op jit(solution)/shard_map/ppermute | solution.py:62
  52.5 6.2 %collective-permute-done.11.refs_6_ = bf16[4,48,1536]{2,1,0:T(8,128)(2,1)S(1)} collective-permute-done((bf16[4,48,1536]{2,1,0:T(8,128)(2,1)S(1)}, bf16[4,48,1536]{2,1,0:T(8,128)(2,1)S(1)}, u32[]{:S(2)}, u32[]{:S(2)}) %collective-permute-start.11) | collective-permute-done | bytes 589856 | tf_op jit(solution)/shard_map/ppermute | solution.py:62
  58.8 5.9 %collective-permute-start.8 = (bf16[4,48,1536]{2,1,0:T(8,128)(2,1)S(1)}, bf16[4,48,1536]{2,1,0:T(8,128)(2,1)S(1)}, u32[]{:S(2)}, u32[]{:S(2)}) collective-permute-start(bf16[4,48,1536]{2,1,0:T(8,128)(2,1)S(1)} %collective-permute-done.4.refs_2_), channel_id=1, source_target_pairs={{0,64},{1,65},{2,66},{3,67},{4,68},{5,69},{6,70},{7,71},{8,72},{9,... | collective-permute-start | bytes 1769480 | tf_op jit(solution)/shard_map/ppermute | solution.py:62
  64.6 5.1 %collective-permute-done.13.refs_8_ = bf16[4,48,1536]{2,1,0:T(8,128)(2,1)S(1)} collective-permute-done((bf16[4,48,1536]{2,1,0:T(8,128)(2,1)S(1)}, bf16[4,48,1536]{2,1,0:T(8,128)(2,1)S(1)}, u32[]{:S(2)}, u32[]{:S(2)}) %collective-permute-start.13) | collective-permute-done | bytes 589856 | tf_op jit(solution)/shard_map/ppermute | solution.py:62
  69.7 8.8 %collective-permute-start.10 = (bf16[4,48,1536]{2,1,0:T(8,128)(2,1)S(1)}, bf16[4,48,1536]{2,1,0:T(8,128)(2,1)S(1)}, u32[]{:S(2)}, u32[]{:S(2)}) collective-permute-start(bf16[4,48,1536]{2,1,0:T(8,128)(2,1)S(1)} %collective-permute-done.9.refs_4_), channel_id=1, source_target_pairs={{0,64},{1,65},{2,66},{3,67},{4,68},{5,69},{6,70},{7,71},{8,72},{9,... | collective-permute-start | bytes 1769480 | tf_op jit(solution)/shard_map/ppermute | solution.py:62
  78.6 2.3 %collective-permute-start.6 = (bf16[2,2,16,1536]{3,2,1,0:T(8,128)(2,1)S(1)}, bf16[2,2,16,1536]{3,2,1,0:T(8,128)(2,1)S(1)}, u32[]{:S(2)}, u32[]{:S(2)}) collective-permute-start(bf16[2,2,16,1536]{3,2,1,0:T(8,128)(2,1)S(1)} %pad_maximum_fusion.3), channel_id=1, source_target_pairs={{64,0},{128,64},{192,128},{65,1},{129,65},{193,129},{66,2},{130,66... | collective-permute-start | bytes 589832 | tf_op jit(solution)/shard_map/ppermute | solution.py:72
  82.1 4.0 %collective-permute-done.6 = bf16[2,2,16,1536]{3,2,1,0:T(8,128)(2,1)S(1)} collective-permute-done((bf16[2,2,16,1536]{3,2,1,0:T(8,128)(2,1)S(1)}, bf16[2,2,16,1536]{3,2,1,0:T(8,128)(2,1)S(1)}, u32[]{:S(2)}, u32[]{:S(2)}) %collective-permute-start.6) | collective-permute-done | bytes 196640 | tf_op jit(solution)/shard_map/ppermute | solution.py:72
  86.1 3.4 %collective-permute-start.17 = (bf16[4,48,1536]{2,1,0:T(8,128)(2,1)S(1)}, bf16[4,48,1536]{2,1,0:T(8,128)(2,1)S(1)}, u32[]{:S(2)}, u32[]{:S(2)}) collective-permute-start(bf16[4,48,1536]{2,1,0:T(8,128)(2,1)S(1)} %collective-permute-done.13.refs_8_), channel_id=1, source_target_pairs={{0,56},{1,57},{2,58},{3,59},{4,60},{5,61},{6,62},{7,63},{8,0},{9,1... | collective-permute-start | bytes 1769480 | tf_op jit(solution)/shard_map/ppermute | solution.py:62
  90.3 7.5 %collective-permute-done.15.refs_10_ = bf16[4,48,1536]{2,1,0:T(8,128)(2,1)} collective-permute-done((bf16[4,48,1536]{2,1,0:T(8,128)(2,1)S(1)}, bf16[4,48,1536]{2,1,0:T(8,128)(2,1)}, u32[]{:S(2)}, u32[]{:S(2)}) %collective-permute-start.15) | collective-permute-done | bytes 589856 | tf_op jit(solution)/shard_map/ppermute | solution.py:62
  97.8 1.7 collective-permute-done.17.refs_12_
  102.0 2.3 %collective-permute-start.21 = (bf16[4,48,768]{2,1,0:T(8,128)(2,1)S(1)}, bf16[4,48,768]{2,1,0:T(8,128)(2,1)}, u32[]{:S(2)}, u32[]{:S(2)}) collective-permute-start(bf16[4,48,768]{2,1,0:T(8,128)(2,1)S(1)} %slice.77), channel_id=1, source_target_pairs={{0,56},{1,57},{2,58},{3,59},{4,60},{5,61},{6,62},{7,63},{8,0},{9,1... | collective-permute-start | bytes 884744 | tf_op jit(solution)/shard_map/ppermute | solution.py:62
  106.8 3.6 %collective-permute-done.19.refs_14_ = bf16[4,48,768]{2,1,0:T(8,128)(2,1)} collective-permute-done((bf16[4,48,768]{2,1,0:T(8,128)(2,1)S(1)}, bf16[4,48,768]{2,1,0:T(8,128)(2,1)}, u32[]{:S(2)}, u32[]{:S(2)}) %collective-permute-start.19) | collective-permute-done | bytes 294944 | tf_op jit(solution)/shard_map/ppermute | solution.py:62
  110.5 1.9 collective-permute-start.33
  115.7 1.8 collective-permute-done.20.refs_15_
  124.3 33.4 %window_attention.1 = bf16[2,256,1536]{2,1,0:T(8,128)(2,1)} custom-call(s32[3]{0:T(128)} %pad_add_fusion.pos, bf16[256,1536]{1,0:T(8,128)(2,1)} %bitcast.33, bf16[256,1536]{1,0:T(8,128)(2,1)} %bitcast.32, f32[256,128]{1,0:T(8,128)} %add_convert_fusion.mask, f32[1,1536]{1,0:T(1,128)} %broadcast_in_dim.18.gain, f32[12,128]{1,0:T(8,128)} %broadcast_in_dim.21.scale, ...), custom_call_target="tpu_custom_call" | custom-call | flops 11000000512 | bytes 24000000 | tf_op jit(solution)/shard_map/window_attention/pallas_call | solution.py:271
  160.2 5.2 %collective-permute-start.40 = (bf16[2,2,8,1536]{3,2,1,0:T(8,128)(2,1)S(1)}, bf16[2,2,8,1536]{3,2,1,0:T(8,128)(2,1)S(1)}, u32[]{:S(2)}, u32[]{:S(2)}) collective-permute-start(bf16[2,2,8,1536]{3,2,1,0:T(8,128)(2,1)S(1)} %get-tuple-element.8), channel_id=1, source_target_pairs={{0,65},{1,66},{2,67},{3,68},{4,69},{5,70},{6,71},{7,72},{8,73},{9,... | collective-permute-start | bytes 294920 | tf_op jit(solution)/shard_map/ppermute | solution.py:62
  165.4 2.5 %collective-permute-start.41 = (bf16[2,2,8,1536]{3,2,1,0:T(8,128)(2,1)S(1)}, bf16[2,2,8,1536]{3,2,1,0:T(8,128)(2,1)S(1)}, u32[]{:S(2)}, u32[]{:S(2)}) collective-permute-start(bf16[2,2,8,1536]{3,2,1,0:T(8,128)(2,1)S(1)} %get-tuple-element.9), channel_id=1, source_target_pairs={{0,64},{64,128},{128,192},{1,65},{65,129},{129,193},{2,66},{66,130... | collective-permute-start | bytes 294920 | tf_op jit(solution)/shard_map/ppermute | solution.py:72
  167.9 16.4 %collective-permute-done.40 = bf16[2,2,8,1536]{3,2,1,0:T(8,128)(2,1)S(1)} collective-permute-done((bf16[2,2,8,1536]{3,2,1,0:T(8,128)(2,1)S(1)}, bf16[2,2,8,1536]{3,2,1,0:T(8,128)(2,1)S(1)}, u32[]{:S(2)}, u32[]{:S(2)}) %collective-permute-start.40) | collective-permute-done | bytes 98336 | tf_op jit(solution)/shard_map/ppermute | solution.py:62
  185.6 2.0 %finish.1 = (bf16[256,1536]{1,0:T(8,128)(2,1)}, bf16[256,1536]{1,0:T(8,128)(2,1)}) custom-call(bf16[256,1536]{1,0:T(8,128)(2,1)S(1)} %bitcast.27, bf16[256,1536]{1,0:T(8,128)(2,1)S(1)} %bitcast.29, bf16[2,256,1536]{2,1,0:T(8,128)(2,1)S(1)} %bitcast.25, f32[1,1536]{1,0:T(1,128)S(1)} %copy-done.2), custom_call_target="tpu_custom_call" | custom-call | tf_op jit(solution)/shard_map/finish/pallas_call | solution.py:310
  (139 shorter events, 27.9 us)
Async XLA Ops:
  5.1 7.7 %collective-permute-start = (bf16[24,1536]{1,0:T(8,128)(2,1)S(1)}, bf16[24,1536]{1,0:T(8,128)(2,1)S(1)}, u32[]{:S(2)}, u32[]{:S(2)}) collective-permute-start(bf16[24,1536]{1,0:T(8,128)(2,1)S(1)} %get-tuple-element.17), channel_id=1, source_target_pairs={{0,129},{1,128},{2,131},{3,130},{4,133},{5,132},{6,135},{7,134},{8... | collective-permute-start | bytes 221192 | tf_op jit(solution)/shard_map/ppermute | solution.py:62
  6.8 21.6 %collective-permute-start.24 = (bf16[1,48,1536]{2,1,0:T(8,128)(2,1)S(1)}, bf16[1,48,1536]{2,1,0:T(8,128)(2,1)S(1)}, u32[]{:S(2)}, u32[]{:S(2)}) collective-permute-start(bf16[1,48,1536]{2,1,0:T(8,128)(2,1)S(1)} %maximum_bitcast_fusion.1), channel_id=1, source_target_pairs={{0,8},{1,9},{2,10},{3,11},{4,12},{5,13},{6,14},{7,15},{8,16},{9,17... | collective-permute-start | bytes 442376 | tf_op jit(solution)/shard_map/ppermute | solution.py:62
  8.7 19.8 %collective-permute-start.25 = (bf16[1,48,1536]{2,1,0:T(8,128)(2,1)S(1)}, bf16[1,48,1536]{2,1,0:T(8,128)(2,1)S(1)}, u32[]{:S(2)}, u32[]{:S(2)}) collective-permute-start(bf16[1,48,1536]{2,1,0:T(8,128)(2,1)S(1)} %maximum_bitcast_fusion.1), channel_id=1, source_target_pairs={{0,56},{1,57},{2,58},{3,59},{4,60},{5,61},{6,62},{7,63},{8,0},{9,1... | collective-permute-start | bytes 442376 | tf_op jit(solution)/shard_map/ppermute | solution.py:62
  15.7 6.5 %collective-permute-start.3 = (bf16[1,48,1536]{2,1,0:T(8,128)(2,1)S(1)}, bf16[1,48,1536]{2,1,0:T(8,128)(2,1)S(1)}, u32[]{:S(2)}, u32[]{:S(2)}) collective-permute-start(bf16[1,48,1536]{2,1,0:T(8,128)(2,1)S(1)} %maximum_bitcast_fusion), channel_id=1, source_target_pairs={{0,4},{1,5},{2,6},{3,7},{4,0},{5,1},{6,2},{7,3},{8,12},{9,13},{10,... | collective-permute-start | bytes 442376 | tf_op jit(solution)/shard_map/ppermute | solution.py:62
  22.3 21.6 %collective-permute-start.4 = (bf16[4,48,1536]{2,1,0:T(8,128)(2,1)S(1)}, bf16[4,48,1536]{2,1,0:T(8,128)(2,1)S(1)}, u32[]{:S(2)}, u32[]{:S(2)}) collective-permute-start(bf16[4,48,1536]{2,1,0:T(8,128)(2,1)S(1)} %pad_maximum_fusion.2.refs_0_), channel_id=1, source_target_pairs={{0,8},{1,9},{2,10},{3,11},{4,12},{5,13},{6,14},{7,15},{8,16},{9,17... | collective-permute-start | bytes 1769480 | tf_op jit(solution)/shard_map/ppermute | solution.py:62
  22.4 25.7 %collective-permute-start.9 = (bf16[4,48,1536]{2,1,0:T(8,128)(2,1)S(1)}, bf16[4,48,1536]{2,1,0:T(8,128)(2,1)S(1)}, u32[]{:S(2)}, u32[]{:S(2)}) collective-permute-start(bf16[4,48,1536]{2,1,0:T(8,128)(2,1)S(1)} %pad_maximum_fusion.2.refs_0_), channel_id=1, source_target_pairs={{0,56},{1,57},{2,58},{3,59},{4,60},{5,61},{6,62},{7,63},{8,0},{9,1... | collective-permute-start | bytes 1769480 | tf_op jit(solution)/shard_map/ppermute | solution.py:62
  25.0 24.8 %collective-permute-start.7 = (bf16[4,48,1536]{2,1,0:T(8,128)(2,1)S(1)}, bf16[4,48,1536]{2,1,0:T(8,128)(2,1)S(1)}, u32[]{:S(2)}, u32[]{:S(2)}) collective-permute-start(bf16[4,48,1536]{2,1,0:T(8,128)(2,1)S(1)} %pad_maximum_fusion.2.refs_0_), channel_id=1, source_target_pairs={{0,64},{1,65},{2,66},{3,67},{4,68},{5,69},{6,70},{7,71},{8,72},{9,... | collective-permute-start | bytes 1769480 | tf_op jit(solution)/shard_map/ppermute | solution.py:62
  28.5 10.2 %collective-permute-start.26 = (bf16[1,48,1536]{2,1,0:T(8,128)(2,1)S(1)}, bf16[1,48,1536]{2,1,0:T(8,128)(2,1)S(1)}, u32[]{:S(2)}, u32[]{:S(2)}) collective-permute-start(bf16[1,48,1536]{2,1,0:T(8,128)(2,1)S(1)} %collective-permute-done.24), channel_id=1, source_target_pairs={{0,8},{1,9},{2,10},{3,11},{4,12},{5,13},{6,14},{7,15},{8,16},{9,17... | collective-permute-start | bytes 442376 | tf_op jit(solution)/shard_map/ppermute | solution.py:62
  28.5 10.2 %collective-permute-start.27 = (bf16[1,48,1536]{2,1,0:T(8,128)(2,1)S(1)}, bf16[1,48,1536]{2,1,0:T(8,128)(2,1)S(1)}, u32[]{:S(2)}, u32[]{:S(2)}) collective-permute-start(bf16[1,48,1536]{2,1,0:T(8,128)(2,1)S(1)} %collective-permute-done.25), channel_id=1, source_target_pairs={{0,56},{1,57},{2,58},{3,59},{4,60},{5,61},{6,62},{7,63},{8,0},{9,1... | collective-permute-start | bytes 442376 | tf_op jit(solution)/shard_map/ppermute | solution.py:62
  43.9 14.8 %collective-permute-start.11 = (bf16[4,48,1536]{2,1,0:T(8,128)(2,1)S(1)}, bf16[4,48,1536]{2,1,0:T(8,128)(2,1)S(1)}, u32[]{:S(2)}, u32[]{:S(2)}) collective-permute-start(bf16[4,48,1536]{2,1,0:T(8,128)(2,1)S(1)} %collective-permute-done.4.refs_2_), channel_id=1, source_target_pairs={{0,8},{1,9},{2,10},{3,11},{4,12},{5,13},{6,14},{7,15},{8,16},{9,17... | collective-permute-start | bytes 1769480 | tf_op jit(solution)/shard_map/ppermute | solution.py:62
  44.0 34.4 %collective-permute-start.5 = (bf16[2,16,8,1536]{3,2,1,0:T(8,128)(2,1)S(1)}, bf16[2,16,8,1536]{3,2,1,0:T(8,128)(2,1)S(1)}, u32[]{:S(2)}, u32[]{:S(2)}) collective-permute-start(bf16[2,16,8,1536]{3,2,1,0:T(8,128)(2,1)S(1)} %get-tuple-element.5), channel_id=1, source_target_pairs={{0,63},{1,0},{2,1},{3,2},{4,3},{5,4},{6,5},{7,6},{8,7},{9,8},{10,9... | collective-permute-start | bytes 2359304 | tf_op jit(solution)/shard_map/ppermute | solution.py:67
  48.1 21.6 %collective-permute-start.13 = (bf16[4,48,1536]{2,1,0:T(8,128)(2,1)S(1)}, bf16[4,48,1536]{2,1,0:T(8,128)(2,1)S(1)}, u32[]{:S(2)}, u32[]{:S(2)}) collective-permute-start(bf16[4,48,1536]{2,1,0:T(8,128)(2,1)S(1)} %collective-permute-done.9.refs_4_), channel_id=1, source_target_pairs={{0,56},{1,57},{2,58},{3,59},{4,60},{5,61},{6,62},{7,63},{8,0},{9,1... | collective-permute-start | bytes 1769480 | tf_op jit(solution)/shard_map/ppermute | solution.py:62
  49.7 39.8 %collective-permute-start.32 = (bf16[8,48,1536]{2,1,0:T(8,128)(2,1)S(1)}, bf16[8,48,1536]{2,1,0:T(8,128)(2,1)S(1)}, u32[]{:S(2)}, u32[]{:S(2)}) collective-permute-start(bf16[8,48,1536]{2,1,0:T(8,128)(2,1)S(1)} %constant_dynamic-update-slice_fusion.refs_18_), channel_id=1, source_target_pairs={{0,2},{1,3},{2,4},{3,5},{4,6},{5,7},{6,0},{7,1},{8,10},{9,11},{10,... | collective-permute-start | bytes 3538952 | tf_op jit(solution)/shard_map/ppermute | solution.py:62
  49.9 39.7 %collective-permute-start.34 = (bf16[8,48,1536]{2,1,0:T(8,128)(2,1)S(1)}, bf16[8,48,1536]{2,1,0:T(8,128)(2,1)S(1)}, u32[]{:S(2)}, u32[]{:S(2)}) collective-permute-start(bf16[8,48,1536]{2,1,0:T(8,128)(2,1)S(1)} %constant_dynamic-update-slice_fusion.refs_18_), channel_id=1, source_target_pairs={{0,6},{1,7},{2,0},{3,1},{4,2},{5,3},{6,4},{7,5},{8,14},{9,15},{10,... | collective-permute-start | bytes 3538952 | tf_op jit(solution)/shard_map/ppermute | solution.py:62
  58.8 19.8 %collective-permute-start.8 = (bf16[4,48,1536]{2,1,0:T(8,128)(2,1)S(1)}, bf16[4,48,1536]{2,1,0:T(8,128)(2,1)S(1)}, u32[]{:S(2)}, u32[]{:S(2)}) collective-permute-start(bf16[4,48,1536]{2,1,0:T(8,128)(2,1)S(1)} %collective-permute-done.4.refs_2_), channel_id=1, source_target_pairs={{0,64},{1,65},{2,66},{3,67},{4,68},{5,69},{6,70},{7,71},{8,72},{9,... | collective-permute-start | bytes 1769480 | tf_op jit(solution)/shard_map/ppermute | solution.py:62
  69.7 11.3 %collective-permute-start.10 = (bf16[4,48,1536]{2,1,0:T(8,128)(2,1)S(1)}, bf16[4,48,1536]{2,1,0:T(8,128)(2,1)S(1)}, u32[]{:S(2)}, u32[]{:S(2)}) collective-permute-start(bf16[4,48,1536]{2,1,0:T(8,128)(2,1)S(1)} %collective-permute-done.9.refs_4_), channel_id=1, source_target_pairs={{0,64},{1,65},{2,66},{3,67},{4,68},{5,69},{6,70},{7,71},{8,72},{9,... | collective-permute-start | bytes 1769480 | tf_op jit(solution)/shard_map/ppermute | solution.py:62
  78.5 23.0 %collective-permute-start.31 = (bf16[8,48,1536]{2,1,0:T(8,128)(2,1)S(1)}, bf16[8,48,1536]{2,1,0:T(8,128)(2,1)S(1)}, u32[]{:S(2)}, u32[]{:S(2)}) collective-permute-start(bf16[8,48,1536]{2,1,0:T(8,128)(2,1)S(1)} %constant_dynamic-update-slice_fusion.refs_18_), channel_id=1, source_target_pairs={{0,64},{1,65},{2,66},{3,67},{4,68},{5,69},{6,70},{7,71},{8,72},{9,... | collective-permute-start | bytes 3538952 | tf_op jit(solution)/shard_map/ppermute | solution.py:62
  78.6 7.5 %collective-permute-start.6 = (bf16[2,2,16,1536]{3,2,1,0:T(8,128)(2,1)S(1)}, bf16[2,2,16,1536]{3,2,1,0:T(8,128)(2,1)S(1)}, u32[]{:S(2)}, u32[]{:S(2)}) collective-permute-start(bf16[2,2,16,1536]{3,2,1,0:T(8,128)(2,1)S(1)} %pad_maximum_fusion.3), channel_id=1, source_target_pairs={{64,0},{128,64},{192,128},{65,1},{129,65},{193,129},{66,2},{130,66... | collective-permute-start | bytes 589832 | tf_op jit(solution)/shard_map/ppermute | solution.py:72
  81.0 16.8 %collective-permute-start.15 = (bf16[4,48,1536]{2,1,0:T(8,128)(2,1)S(1)}, bf16[4,48,1536]{2,1,0:T(8,128)(2,1)}, u32[]{:S(2)}, u32[]{:S(2)}) collective-permute-start(bf16[4,48,1536]{2,1,0:T(8,128)(2,1)S(1)} %collective-permute-done.11.refs_6_), channel_id=1, source_target_pairs={{0,8},{1,9},{2,10},{3,11},{4,12},{5,13},{6,14},{7,15},{8,16},{9,17... | collective-permute-start | bytes 1769480 | tf_op jit(solution)/shard_map/ppermute | solution.py:62
  86.1 13.4 %collective-permute-start.17 = (bf16[4,48,1536]{2,1,0:T(8,128)(2,1)S(1)}, bf16[4,48,1536]{2,1,0:T(8,128)(2,1)S(1)}, u32[]{:S(2)}, u32[]{:S(2)}) collective-permute-start(bf16[4,48,1536]{2,1,0:T(8,128)(2,1)S(1)} %collective-permute-done.13.refs_8_), channel_id=1, source_target_pairs={{0,56},{1,57},{2,58},{3,59},{4,60},{5,61},{6,62},{7,63},{8,0},{9,1... | collective-permute-start | bytes 1769480 | tf_op jit(solution)/shard_map/ppermute | solution.py:62
  89.5 12.5 %collective-permute-start.12 = (bf16[4,48,1536]{2,1,0:T(8,128)(2,1)S(1)}, bf16[4,48,1536]{2,1,0:T(8,128)(2,1)S(1)}, u32[]{:S(2)}, u32[]{:S(2)}) collective-permute-start(bf16[4,48,1536]{2,1,0:T(8,128)(2,1)S(1)} %collective-permute-done.11.refs_6_), channel_id=1, source_target_pairs={{0,64},{1,65},{2,66},{3,67},{4,68},{5,69},{6,70},{7,71},{8,72},{9,... | collective-permute-start | bytes 1769480 | tf_op jit(solution)/shard_map/ppermute | solution.py:62
  89.6 14.7 %collective-permute-start.14 = (bf16[4,48,1536]{2,1,0:T(8,128)(2,1)S(1)}, bf16[4,48,1536]{2,1,0:T(8,128)(2,1)S(1)}, u32[]{:S(2)}, u32[]{:S(2)}) collective-permute-start(bf16[4,48,1536]{2,1,0:T(8,128)(2,1)S(1)} %collective-permute-done.13.refs_8_), channel_id=1, source_target_pairs={{0,64},{1,65},{2,66},{3,67},{4,68},{5,69},{6,70},{7,71},{8,72},{9,... | collective-permute-start | bytes 1769480 | tf_op jit(solution)/shard_map/ppermute | solution.py:62
  97.8 15.8 %collective-permute-start.36 = (bf16[8,48,768]{2,1,0:T(8,128)(2,1)S(1)}, bf16[8,48,768]{2,1,0:T(8,128)(2,1)}, u32[]{:S(2)}, u32[]{:S(2)}) collective-permute-start(bf16[8,48,768]{2,1,0:T(8,128)(2,1)S(1)} %slice.78), channel_id=1, source_target_pairs={{0,2},{1,3},{2,4},{3,5},{4,6},{5,7},{6,0},{7,1},{8,10},{9,11},{10,... | collective-permute-start | bytes 1769480 | tf_op jit(solution)/shard_map/ppermute | solution.py:62
  99.5 15.4 %collective-permute-start.38 = (bf16[8,48,768]{2,1,0:T(8,128)(2,1)S(1)}, bf16[8,48,768]{2,1,0:T(8,128)(2,1)}, u32[]{:S(2)}, u32[]{:S(2)}) collective-permute-start(bf16[8,48,768]{2,1,0:T(8,128)(2,1)S(1)} %slice.79), channel_id=1, source_target_pairs={{0,6},{1,7},{2,0},{3,1},{4,2},{5,3},{6,4},{7,5},{8,14},{9,15},{10,... | collective-permute-start | bytes 1769480 | tf_op jit(solution)/shard_map/ppermute | solution.py:62
  101.5 9.0 %collective-permute-start.19 = (bf16[4,48,768]{2,1,0:T(8,128)(2,1)S(1)}, bf16[4,48,768]{2,1,0:T(8,128)(2,1)}, u32[]{:S(2)}, u32[]{:S(2)}) collective-permute-start(bf16[4,48,768]{2,1,0:T(8,128)(2,1)S(1)} %slice.76), channel_id=1, source_target_pairs={{0,8},{1,9},{2,10},{3,11},{4,12},{5,13},{6,14},{7,15},{8,16},{9,17... | collective-permute-start | bytes 884744 | tf_op jit(solution)/shard_map/ppermute | solution.py:62
  102.0 10.3 %collective-permute-start.21 = (bf16[4,48,768]{2,1,0:T(8,128)(2,1)S(1)}, bf16[4,48,768]{2,1,0:T(8,128)(2,1)}, u32[]{:S(2)}, u32[]{:S(2)}) collective-permute-start(bf16[4,48,768]{2,1,0:T(8,128)(2,1)S(1)} %slice.77), channel_id=1, source_target_pairs={{0,56},{1,57},{2,58},{3,59},{4,60},{5,61},{6,62},{7,63},{8,0},{9,1... | collective-permute-start | bytes 884744 | tf_op jit(solution)/shard_map/ppermute | solution.py:62
  105.2 12.9 %collective-permute-start.16 = (bf16[4,48,1536]{2,1,0:T(8,128)(2,1)}, bf16[4,48,1536]{2,1,0:T(8,128)(2,1)}, u32[]{:S(2)}, u32[]{:S(2)}) collective-permute-start(bf16[4,48,1536]{2,1,0:T(8,128)(2,1)} %collective-permute-done.15.refs_10_), channel_id=1, source_target_pairs={{0,64},{1,65},{2,66},{3,67},{4,68},{5,69},{6,70},{7,71},{8,72},{9,... | collective-permute-start | bytes 1769480 | tf_op jit(solution)/shard_map/ppermute | solution.py:62
  110.5 12.8 %collective-permute-start.33 = (bf16[8,48,1536]{2,1,0:T(8,128)(2,1)}, bf16[8,48,1536]{2,1,0:T(8,128)(2,1)}, u32[]{:S(2)}, u32[]{:S(2)}) collective-permute-start(bf16[8,48,1536]{2,1,0:T(8,128)(2,1)} %copy-done.4), channel_id=1, source_target_pairs={{0,64},{1,65},{2,66},{3,67},{4,68},{5,69},{6,70},{7,71},{8,72},{9,... | collective-permute-start | bytes 3538952 | tf_op jit(solution)/shard_map/ppermute | solution.py:62
  112.3 11.0 %collective-permute-start.35 = (bf16[8,48,1536]{2,1,0:T(8,128)(2,1)}, bf16[8,48,1536]{2,1,0:T(8,128)(2,1)}, u32[]{:S(2)}, u32[]{:S(2)}) collective-permute-start(bf16[8,48,1536]{2,1,0:T(8,128)(2,1)} %copy-done.5), channel_id=1, source_target_pairs={{0,64},{1,65},{2,66},{3,67},{4,68},{5,69},{6,70},{7,71},{8,72},{9,... | collective-permute-start | bytes 3538952 | tf_op jit(solution)/shard_map/ppermute | solution.py:62
  159.1 25.1 %collective-permute-start.42 = (bf16[2,14,8,1536]{3,2,1,0:T(8,128)(2,1)S(1)}, bf16[2,14,8,1536]{3,2,1,0:T(8,128)(2,1)S(1)}, u32[]{:S(2)}, u32[]{:S(2)}) collective-permute-start(bf16[2,14,8,1536]{3,2,1,0:T(8,128)(2,1)S(1)} %get-tuple-element.10), channel_id=1, source_target_pairs={{0,1},{1,2},{2,3},{3,4},{4,5},{5,6},{6,7},{7,8},{8,9},{9,10},{10,1... | collective-permute-start | bytes 2064392 | tf_op jit(solution)/shard_map/ppermute | solution.py:67
  160.2 24.1 %collective-permute-start.40 = (bf16[2,2,8,1536]{3,2,1,0:T(8,128)(2,1)S(1)}, bf16[2,2,8,1536]{3,2,1,0:T(8,128)(2,1)S(1)}, u32[]{:S(2)}, u32[]{:S(2)}) collective-permute-start(bf16[2,2,8,1536]{3,2,1,0:T(8,128)(2,1)S(1)} %get-tuple-element.8), channel_id=1, source_target_pairs={{0,65},{1,66},{2,67},{3,68},{4,69},{5,70},{6,71},{7,72},{8,73},{9,... | collective-permute-start | bytes 294920 | tf_op jit(solution)/shard_map/ppermute | solution.py:62
  165.4 18.8 %collective-permute-start.41 = (bf16[2,2,8,1536]{3,2,1,0:T(8,128)(2,1)S(1)}, bf16[2,2,8,1536]{3,2,1,0:T(8,128)(2,1)S(1)}, u32[]{:S(2)}, u32[]{:S(2)}) collective-permute-start(bf16[2,2,8,1536]{3,2,1,0:T(8,128)(2,1)S(1)} %get-tuple-element.9), channel_id=1, source_target_pairs={{0,64},{64,128},{128,192},{1,65},{65,129},{129,193},{2,66},{66,130... | collective-permute-start | bytes 294920 | tf_op jit(solution)/shard_map/ppermute | solution.py:72
  (33 other events, 439.2 us)
where the time goes:
time: 188 us
  starting transfers between devices  72.9 us (39%)
  waiting for transfers between devices  62.7 us (33%)
  Pallas kernels  35.4 us (19%)
  local copies, waits for them, and re-layouts  9.68 us (5%)
  other arithmetic  5.78 us (3%)
    ppermute x39, starting transfers between devices, send(): return lax.ppermute(value, AXES, pairs)  64 us
    ppermute x39, waiting for transfers between devices, send(): return lax.ppermute(value, AXES, pairs)  58.6 us
    pallas_call x1, Pallas kernels, window_attention(): pl.pallas_call(functools.partial(window_kernel, plan), out_shape=jax.Shap...  33.4 us
    ppermute x2, starting transfers between devices, lat_line(): lax.ppermute(value, LAT, [(i, i + step) for i in range(size) if 0 <= i +...  4.79 us
    ppermute x2, starting transfers between devices, lon_ring(): lax.ppermute(value, LON, [(i, (i + step) % size) for i in range(size)])  4.11 us
    ppermute x2, waiting for transfers between devices, lat_line(): lax.ppermute(value, LAT, [(i, i + step) for i in range(size) if 0 <= i +...  4.04 us
  transfers between devices with their start and end apart: 43, of which 15 were waited for; matrix products, arithmetic and copies ran while one was open for 5% of the time, Pallas kernels for 0%

commit v1 on v0

--- a/solution.py
+++ b/solution.py
@@ -166,18 +166,35 @@
     return mm(jnp.concatenate([high, low], axis=1), ones)
 
 
+def arrived(ref, sem):
+    pltpu.make_async_copy(ref, ref, sem).wait()
+
+
+def fetch(plan, blocks, weights, sem, z, y, core):
+    def copy(sibling, side):
+        for (distances, column, other), block in zip(plan, blocks):
+            if other != sibling:
+                continue
+            cols = pl.ds(column, block.shape[2])
+            for j, (dz, dy) in enumerate(distances):
+                unit = lax.rem(z - dz + 8, 8) * 4 + lax.rem(y - dy + 4, 4)
+                pltpu.make_async_copy(block.at[j], weights.at[side, unit, :, cols], sem.at[side]).start()
+
+    for mine in (0, 1):
+
+        @pl.when(core == mine)
+        def _(mine=mine):
+            copy(1 - mine, 1)
+            copy(mine, 0)
+
+
 def window_kernel(plan, pos, xs, gs, mask, gain, scale, *refs):
     count = len(plan)
     blocks = refs[:count]
     result, weights, normed, gatt, packed, attended, sem = refs[count:]
     z, y, core = pos[0], pos[1], pos[2]
 
-    for (distances, column, sibling), block in zip(plan, blocks):
-        side = lax.rem(core + sibling, 2)
-        cols = pl.ds(column, block.shape[2])
-        for j, (dz, dy) in enumerate(distances):
-            unit = lax.rem(z - dz + 8, 8) * 4 + lax.rem(y - dy + 4, 4)
-            pltpu.make_async_copy(block.at[j], weights.at[side, unit, :, cols], sem.at[side]).start()
+    fetch(plan, blocks, weights, sem, z, y, core)
 
     for i in range(4):
         rows = pl.ds(i * WIN, WIN)
@@ -186,15 +203,16 @@
         spread = jnp.mean(centre * centre, axis=-1, keepdims=True)
         normed[rows, :] = bf(centre * lax.rsqrt(spread + 1e-05) * gain[...])
 
-    for side in (1, 0):
-        pltpu.make_async_copy(weights.at[side], weights.at[side], sem.at[side]).wait()
+    arrived(weights.at[1], sem.at[1])
 
     @pl.loop(0, 2)
     def _(i):
         w = weights[1, pl.ds(i * 16, 16), :, D:].reshape(768, D)
         gatt[:, pl.ds(pl.multiple_of(i * 768, 128), 768)] = bf(mm_nt(gs[...], w))
 
-    for m in range(3):
+    for m in (2, 0, 1):
+        if m == 0:
+            arrived(weights.at[0], sem.at[0])
 
         @pl.loop(0, 3)
         def _(i, m=m):

time: 188 us -> 185 us (0.984)
  Pallas kernels: 35.4 us -> 32.8 us
    pallas_call x1, Pallas kernels: 33.4 us -> 30.8 us  [window_attention(): pl.pallas_call(functools.partial(window_kernel, plan), out_shape=jax.Shap...]
where the time goes in v1:
time: 185 us
  starting transfers between devices  72.9 us (39%)
  waiting for transfers between devices  62.7 us (34%)
  Pallas kernels  32.8 us (18%)
  local copies, waits for them, and re-layouts  9.68 us (5%)
  other arithmetic  5.78 us (3%)
    ppermute x39, starting transfers between devices, send(): return lax.ppermute(value, AXES, pairs)  64 us
    ppermute x39, waiting for transfers between devices, send(): return lax.ppermute(value, AXES, pairs)  58.6 us
    pallas_call x1, Pallas kernels, window_attention(): pl.pallas_call(functools.partial(window_kernel, plan), out_shape=jax.Shap...  30.8 us
    ppermute x2, starting transfers between devices, lat_line(): lax.ppermute(value, LAT, [(i, i + step) for i in range(size) if 0 <= i +...  4.79 us
    ppermute x2, starting transfers between devices, lon_ring(): lax.ppermute(value, LON, [(i, (i + step) % size) for i in range(size)])  4.11 us
    ppermute x2, waiting for transfers between devices, lat_line(): lax.ppermute(value, LAT, [(i, i + step) for i in range(size) if 0 <= i +...  4.04 us
  transfers between devices with their start and end apart: 43, of which 15 were waited for; matrix products, arithmetic and copies ran while one was open for 5% of the time, Pallas kernels for 0%

profile of v1, /device:TPU:1, one launch (start us, length us, event | category | flops | bytes accessed | tf_op | source)
XLA Modules:
  0.0 185.0 jit_solution(10172150895725722635)
XLA Ops:
  1.7 3.4 %collective-permute-start.23 = (bf16[24,1536]{1,0:T(8,128)(2,1)S(1)}, bf16[24,1536]{1,0:T(8,128)(2,1)S(1)}, u32[]{:S(2)}, u32[]{:S(2)}) collective-permute-start(bf16[24,1536]{1,0:T(8,128)(2,1)S(1)} %get-tuple-element.16), channel_id=1, source_target_pairs={{0,129},{1,128},{2,131},{3,130},{4,133},{5,132},{6,135},{7,134},{8... | collective-permute-start | bytes 221192 | tf_op jit(solution)/shard_map/ppermute | solution.py:62
  6.8 1.9 %collective-permute-start.24 = (bf16[1,48,1536]{2,1,0:T(8,128)(2,1)S(1)}, bf16[1,48,1536]{2,1,0:T(8,128)(2,1)S(1)}, u32[]{:S(2)}, u32[]{:S(2)}) collective-permute-start(bf16[1,48,1536]{2,1,0:T(8,128)(2,1)S(1)} %maximum_bitcast_fusion.1), channel_id=1, source_target_pairs={{0,8},{1,9},{2,10},{3,11},{4,12},{5,13},{6,14},{7,15},{8,16},{9,17... | collective-permute-start | bytes 442376 | tf_op jit(solution)/shard_map/ppermute | solution.py:62
  8.7 4.0 %collective-permute-start.25 = (bf16[1,48,1536]{2,1,0:T(8,128)(2,1)S(1)}, bf16[1,48,1536]{2,1,0:T(8,128)(2,1)S(1)}, u32[]{:S(2)}, u32[]{:S(2)}) collective-permute-start(bf16[1,48,1536]{2,1,0:T(8,128)(2,1)S(1)} %maximum_bitcast_fusion.1), channel_id=1, source_target_pairs={{0,56},{1,57},{2,58},{3,59},{4,60},{5,61},{6,62},{7,63},{8,0},{9,1... | collective-permute-start | bytes 442376 | tf_op jit(solution)/shard_map/ppermute | solution.py:62
  14.2 1.5 collective-permute-start.2
  15.7 1.6 collective-permute-start.3
  18.2 4.0 %collective-permute-done.3 = bf16[1,48,1536]{2,1,0:T(8,128)(2,1)S(1)} collective-permute-done((bf16[1,48,1536]{2,1,0:T(8,128)(2,1)S(1)}, bf16[1,48,1536]{2,1,0:T(8,128)(2,1)S(1)}, u32[]{:S(2)}, u32[]{:S(2)}) %collective-permute-start.3) | collective-permute-done | bytes 147488 | tf_op jit(solution)/shard_map/ppermute | solution.py:62
  22.4 2.7 %collective-permute-start.9 = (bf16[4,48,1536]{2,1,0:T(8,128)(2,1)S(1)}, bf16[4,48,1536]{2,1,0:T(8,128)(2,1)S(1)}, u32[]{:S(2)}, u32[]{:S(2)}) collective-permute-start(bf16[4,48,1536]{2,1,0:T(8,128)(2,1)S(1)} %pad_maximum_fusion.2.refs_0_), channel_id=1, source_target_pairs={{0,56},{1,57},{2,58},{3,59},{4,60},{5,61},{6,62},{7,63},{8,0},{9,1... | collective-permute-start | bytes 1769480 | tf_op jit(solution)/shard_map/ppermute | solution.py:62
  25.0 3.4 %collective-permute-start.7 = (bf16[4,48,1536]{2,1,0:T(8,128)(2,1)S(1)}, bf16[4,48,1536]{2,1,0:T(8,128)(2,1)S(1)}, u32[]{:S(2)}, u32[]{:S(2)}) collective-permute-start(bf16[4,48,1536]{2,1,0:T(8,128)(2,1)S(1)} %pad_maximum_fusion.2.refs_0_), channel_id=1, source_target_pairs={{0,64},{1,65},{2,66},{3,67},{4,68},{5,69},{6,70},{7,71},{8,72},{9,... | collective-permute-start | bytes 1769480 | tf_op jit(solution)/shard_map/ppermute | solution.py:62
  28.5 2.7 %collective-permute-start.27 = (bf16[1,48,1536]{2,1,0:T(8,128)(2,1)S(1)}, bf16[1,48,1536]{2,1,0:T(8,128)(2,1)S(1)}, u32[]{:S(2)}, u32[]{:S(2)}) collective-permute-start(bf16[1,48,1536]{2,1,0:T(8,128)(2,1)S(1)} %collective-permute-done.25), channel_id=1, source_target_pairs={{0,56},{1,57},{2,58},{3,59},{4,60},{5,61},{6,62},{7,63},{8,0},{9,1... | collective-permute-start | bytes 442376 | tf_op jit(solution)/shard_map/ppermute | solution.py:62
  31.3 7.4 %collective-permute-done.26 = bf16[1,48,1536]{2,1,0:T(8,128)(2,1)S(1)} collective-permute-done((bf16[1,48,1536]{2,1,0:T(8,128)(2,1)S(1)}, bf16[1,48,1536]{2,1,0:T(8,128)(2,1)S(1)}, u32[]{:S(2)}, u32[]{:S(2)}) %collective-permute-start.26) | collective-permute-done | bytes 147488 | tf_op jit(solution)/shard_map/ppermute | solution.py:62
  38.7 2.7 %collective-permute-start.29 = (bf16[1,48,1536]{2,1,0:T(8,128)(2,1)S(1)}, bf16[1,48,1536]{2,1,0:T(8,128)(2,1)S(1)}, u32[]{:S(2)}, u32[]{:S(2)}) collective-permute-start(bf16[1,48,1536]{2,1,0:T(8,128)(2,1)S(1)} %collective-permute-done.27), channel_id=1, source_target_pairs={{0,56},{1,57},{2,58},{3,59},{4,60},{5,61},{6,62},{7,63},{8,0},{9,1... | collective-permute-start | bytes 442376 | tf_op jit(solution)/shard_map/ppermute | solution.py:62
  41.4 2.5 %collective-permute-done.28 = bf16[1,48,1536]{2,1,0:T(8,128)(2,1)S(1)} collective-permute-done((bf16[1,48,1536]{2,1,0:T(8,128)(2,1)S(1)}, bf16[1,48,1536]{2,1,0:T(8,128)(2,1)S(1)}, u32[]{:S(2)}, u32[]{:S(2)}) %collective-permute-start.28) | collective-permute-done | bytes 147488 | tf_op jit(solution)/shard_map/ppermute | solution.py:62
  44.0 4.0 %collective-permute-start.5 = (bf16[2,16,8,1536]{3,2,1,0:T(8,128)(2,1)S(1)}, bf16[2,16,8,1536]{3,2,1,0:T(8,128)(2,1)S(1)}, u32[]{:S(2)}, u32[]{:S(2)}) collective-permute-start(bf16[2,16,8,1536]{3,2,1,0:T(8,128)(2,1)S(1)} %get-tuple-element.5), channel_id=1, source_target_pairs={{0,63},{1,0},{2,1},{3,2},{4,3},{5,4},{6,5},{7,6},{8,7},{9,8},{10,9... | collective-permute-start | bytes 2359304 | tf_op jit(solution)/shard_map/ppermute | solution.py:67
  49.9 2.6 %collective-permute-start.34 = (bf16[8,48,1536]{2,1,0:T(8,128)(2,1)S(1)}, bf16[8,48,1536]{2,1,0:T(8,128)(2,1)S(1)}, u32[]{:S(2)}, u32[]{:S(2)}) collective-permute-start(bf16[8,48,1536]{2,1,0:T(8,128)(2,1)S(1)} %constant_dynamic-update-slice_fusion.refs_18_), channel_id=1, source_target_pairs={{0,6},{1,7},{2,0},{3,1},{4,2},{5,3},{6,4},{7,5},{8,14},{9,15},{10,... | collective-permute-start | bytes 3538952 | tf_op jit(solution)/shard_map/ppermute | solution.py:62
  52.5 6.2 %collective-permute-done.11.refs_6_ = bf16[4,48,1536]{2,1,0:T(8,128)(2,1)S(1)} collective-permute-done((bf16[4,48,1536]{2,1,0:T(8,128)(2,1)S(1)}, bf16[4,48,1536]{2,1,0:T(8,128)(2,1)S(1)}, u32[]{:S(2)}, u32[]{:S(2)}) %collective-permute-start.11) | collective-permute-done | bytes 589856 | tf_op jit(solution)/shard_map/ppermute | solution.py:62
  58.8 5.9 %collective-permute-start.8 = (bf16[4,48,1536]{2,1,0:T(8,128)(2,1)S(1)}, bf16[4,48,1536]{2,1,0:T(8,128)(2,1)S(1)}, u32[]{:S(2)}, u32[]{:S(2)}) collective-permute-start(bf16[4,48,1536]{2,1,0:T(8,128)(2,1)S(1)} %collective-permute-done.4.refs_2_), channel_id=1, source_target_pairs={{0,64},{1,65},{2,66},{3,67},{4,68},{5,69},{6,70},{7,71},{8,72},{9,... | collective-permute-start | bytes 1769480 | tf_op jit(solution)/shard_map/ppermute | solution.py:62
  64.6 5.1 %collective-permute-done.13.refs_8_ = bf16[4,48,1536]{2,1,0:T(8,128)(2,1)S(1)} collective-permute-done((bf16[4,48,1536]{2,1,0:T(8,128)(2,1)S(1)}, bf16[4,48,1536]{2,1,0:T(8,128)(2,1)S(1)}, u32[]{:S(2)}, u32[]{:S(2)}) %collective-permute-start.13) | collective-permute-done | bytes 589856 | tf_op jit(solution)/shard_map/ppermute | solution.py:62
  69.7 8.8 %collective-permute-start.10 = (bf16[4,48,1536]{2,1,0:T(8,128)(2,1)S(1)}, bf16[4,48,1536]{2,1,0:T(8,128)(2,1)S(1)}, u32[]{:S(2)}, u32[]{:S(2)}) collective-permute-start(bf16[4,48,1536]{2,1,0:T(8,128)(2,1)S(1)} %collective-permute-done.9.refs_4_), channel_id=1, source_target_pairs={{0,64},{1,65},{2,66},{3,67},{4,68},{5,69},{6,70},{7,71},{8,72},{9,... | collective-permute-start | bytes 1769480 | tf_op jit(solution)/shard_map/ppermute | solution.py:62
  78.6 2.3 %collective-permute-start.6 = (bf16[2,2,16,1536]{3,2,1,0:T(8,128)(2,1)S(1)}, bf16[2,2,16,1536]{3,2,1,0:T(8,128)(2,1)S(1)}, u32[]{:S(2)}, u32[]{:S(2)}) collective-permute-start(bf16[2,2,16,1536]{3,2,1,0:T(8,128)(2,1)S(1)} %pad_maximum_fusion.3), channel_id=1, source_target_pairs={{64,0},{128,64},{192,128},{65,1},{129,65},{193,129},{66,2},{130,66... | collective-permute-start | bytes 589832 | tf_op jit(solution)/shard_map/ppermute | solution.py:72
  82.1 4.0 %collective-permute-done.6 = bf16[2,2,16,1536]{3,2,1,0:T(8,128)(2,1)S(1)} collective-permute-done((bf16[2,2,16,1536]{3,2,1,0:T(8,128)(2,1)S(1)}, bf16[2,2,16,1536]{3,2,1,0:T(8,128)(2,1)S(1)}, u32[]{:S(2)}, u32[]{:S(2)}) %collective-permute-start.6) | collective-permute-done | bytes 196640 | tf_op jit(solution)/shard_map/ppermute | solution.py:72
  86.1 3.4 %collective-permute-start.17 = (bf16[4,48,1536]{2,1,0:T(8,128)(2,1)S(1)}, bf16[4,48,1536]{2,1,0:T(8,128)(2,1)S(1)}, u32[]{:S(2)}, u32[]{:S(2)}) collective-permute-start(bf16[4,48,1536]{2,1,0:T(8,128)(2,1)S(1)} %collective-permute-done.13.refs_8_), channel_id=1, source_target_pairs={{0,56},{1,57},{2,58},{3,59},{4,60},{5,61},{6,62},{7,63},{8,0},{9,1... | collective-permute-start | bytes 1769480 | tf_op jit(solution)/shard_map/ppermute | solution.py:62
  90.3 7.5 %collective-permute-done.15.refs_10_ = bf16[4,48,1536]{2,1,0:T(8,128)(2,1)} collective-permute-done((bf16[4,48,1536]{2,1,0:T(8,128)(2,1)S(1)}, bf16[4,48,1536]{2,1,0:T(8,128)(2,1)}, u32[]{:S(2)}, u32[]{:S(2)}) %collective-permute-start.15) | collective-permute-done | bytes 589856 | tf_op jit(solution)/shard_map/ppermute | solution.py:62
  97.8 1.7 collective-permute-done.17.refs_12_
  102.0 2.3 %collective-permute-start.21 = (bf16[4,48,768]{2,1,0:T(8,128)(2,1)S(1)}, bf16[4,48,768]{2,1,0:T(8,128)(2,1)}, u32[]{:S(2)}, u32[]{:S(2)}) collective-permute-start(bf16[4,48,768]{2,1,0:T(8,128)(2,1)S(1)} %slice.77), channel_id=1, source_target_pairs={{0,56},{1,57},{2,58},{3,59},{4,60},{5,61},{6,62},{7,63},{8,0},{9,1... | collective-permute-start | bytes 884744 | tf_op jit(solution)/shard_map/ppermute | solution.py:62
  106.8 3.6 %collective-permute-done.19.refs_14_ = bf16[4,48,768]{2,1,0:T(8,128)(2,1)} collective-permute-done((bf16[4,48,768]{2,1,0:T(8,128)(2,1)S(1)}, bf16[4,48,768]{2,1,0:T(8,128)(2,1)}, u32[]{:S(2)}, u32[]{:S(2)}) %collective-permute-start.19) | collective-permute-done | bytes 294944 | tf_op jit(solution)/shard_map/ppermute | solution.py:62
  110.5 1.9 %collective-permute-start.33 = (bf16[8,48,1536]{2,1,0:T(8,128)(2,1)}, bf16[8,48,1536]{2,1,0:T(8,128)(2,1)}, u32[]{:S(2)}, u32[]{:S(2)}) collective-permute-start(bf16[8,48,1536]{2,1,0:T(8,128)(2,1)} %copy-done.4), channel_id=1, source_target_pairs={{0,64},{1,65},{2,66},{3,67},{4,68},{5,69},{6,70},{7,71},{8,72},{9,... | collective-permute-start | bytes 3538952 | tf_op jit(solution)/shard_map/ppermute | solution.py:62
  115.7 1.8 collective-permute-done.20.refs_15_
  124.3 30.8 %window_attention.1 = bf16[2,256,1536]{2,1,0:T(8,128)(2,1)} custom-call(s32[3]{0:T(128)} %pad_add_fusion.pos, bf16[256,1536]{1,0:T(8,128)(2,1)} %bitcast.33, bf16[256,1536]{1,0:T(8,128)(2,1)} %bitcast.32, f32[256,128]{1,0:T(8,128)} %add_convert_fusion.mask, f32[1,1536]{1,0:T(1,128)} %broadcast_in_dim.18.gain, f32[12,128]{1,0:T(8,128)} %broadcast_in_dim.21.scale, ...), custom_call_target="tpu_custom_call" | custom-call | flops 11000000512 | bytes 24000000 | tf_op jit(solution)/shard_map/window_attention/pallas_call | solution.py:289
  157.5 5.2 %collective-permute-start.40 = (bf16[2,2,8,1536]{3,2,1,0:T(8,128)(2,1)S(1)}, bf16[2,2,8,1536]{3,2,1,0:T(8,128)(2,1)S(1)}, u32[]{:S(2)}, u32[]{:S(2)}) collective-permute-start(bf16[2,2,8,1536]{3,2,1,0:T(8,128)(2,1)S(1)} %get-tuple-element.8), channel_id=1, source_target_pairs={{0,65},{1,66},{2,67},{3,68},{4,69},{5,70},{6,71},{7,72},{8,73},{9,... | collective-permute-start | bytes 294920 | tf_op jit(solution)/shard_map/ppermute | solution.py:62
  162.8 2.5 %collective-permute-start.41 = (bf16[2,2,8,1536]{3,2,1,0:T(8,128)(2,1)S(1)}, bf16[2,2,8,1536]{3,2,1,0:T(8,128)(2,1)S(1)}, u32[]{:S(2)}, u32[]{:S(2)}) collective-permute-start(bf16[2,2,8,1536]{3,2,1,0:T(8,128)(2,1)S(1)} %get-tuple-element.9), channel_id=1, source_target_pairs={{0,64},{64,128},{128,192},{1,65},{65,129},{129,193},{2,66},{66,130... | collective-permute-start | bytes 294920 | tf_op jit(solution)/shard_map/ppermute | solution.py:72
  165.2 16.4 %collective-permute-done.40 = bf16[2,2,8,1536]{3,2,1,0:T(8,128)(2,1)S(1)} collective-permute-done((bf16[2,2,8,1536]{3,2,1,0:T(8,128)(2,1)S(1)}, bf16[2,2,8,1536]{3,2,1,0:T(8,128)(2,1)S(1)}, u32[]{:S(2)}, u32[]{:S(2)}) %collective-permute-start.40) | collective-permute-done | bytes 98336 | tf_op jit(solution)/shard_map/ppermute | solution.py:62
  183.0 2.0 %finish.1 = (bf16[256,1536]{1,0:T(8,128)(2,1)}, bf16[256,1536]{1,0:T(8,128)(2,1)}) custom-call(bf16[256,1536]{1,0:T(8,128)(2,1)S(1)} %bitcast.27, bf16[256,1536]{1,0:T(8,128)(2,1)S(1)} %bitcast.29, bf16[2,256,1536]{2,1,0:T(8,128)(2,1)S(1)} %bitcast.25, f32[1,1536]{1,0:T(1,128)S(1)} %copy-done.2), custom_call_target="tpu_custom_call" | custom-call | tf_op jit(solution)/shard_map/finish/pallas_call | solution.py:328
  (139 shorter events, 27.9 us)
Async XLA Ops:
  5.1 7.7 %collective-permute-start = (bf16[24,1536]{1,0:T(8,128)(2,1)S(1)}, bf16[24,1536]{1,0:T(8,128)(2,1)S(1)}, u32[]{:S(2)}, u32[]{:S(2)}) collective-permute-start(bf16[24,1536]{1,0:T(8,128)(2,1)S(1)} %get-tuple-element.17), channel_id=1, source_target_pairs={{0,129},{1,128},{2,131},{3,130},{4,133},{5,132},{6,135},{7,134},{8... | collective-permute-start | bytes 221192 | tf_op jit(solution)/shard_map/ppermute | solution.py:62
  6.8 21.6 %collective-permute-start.24 = (bf16[1,48,1536]{2,1,0:T(8,128)(2,1)S(1)}, bf16[1,48,1536]{2,1,0:T(8,128)(2,1)S(1)}, u32[]{:S(2)}, u32[]{:S(2)}) collective-permute-start(bf16[1,48,1536]{2,1,0:T(8,128)(2,1)S(1)} %maximum_bitcast_fusion.1), channel_id=1, source_target_pairs={{0,8},{1,9},{2,10},{3,11},{4,12},{5,13},{6,14},{7,15},{8,16},{9,17... | collective-permute-start | bytes 442376 | tf_op jit(solution)/shard_map/ppermute | solution.py:62
  8.7 19.8 %collective-permute-start.25 = (bf16[1,48,1536]{2,1,0:T(8,128)(2,1)S(1)}, bf16[1,48,1536]{2,1,0:T(8,128)(2,1)S(1)}, u32[]{:S(2)}, u32[]{:S(2)}) collective-permute-start(bf16[1,48,1536]{2,1,0:T(8,128)(2,1)S(1)} %maximum_bitcast_fusion.1), channel_id=1, source_target_pairs={{0,56},{1,57},{2,58},{3,59},{4,60},{5,61},{6,62},{7,63},{8,0},{9,1... | collective-permute-start | bytes 442376 | tf_op jit(solution)/shard_map/ppermute | solution.py:62
  15.7 6.5 %collective-permute-start.3 = (bf16[1,48,1536]{2,1,0:T(8,128)(2,1)S(1)}, bf16[1,48,1536]{2,1,0:T(8,128)(2,1)S(1)}, u32[]{:S(2)}, u32[]{:S(2)}) collective-permute-start(bf16[1,48,1536]{2,1,0:T(8,128)(2,1)S(1)} %maximum_bitcast_fusion), channel_id=1, source_target_pairs={{0,4},{1,5},{2,6},{3,7},{4,0},{5,1},{6,2},{7,3},{8,12},{9,13},{10,... | collective-permute-start | bytes 442376 | tf_op jit(solution)/shard_map/ppermute | solution.py:62
  22.3 21.6 %collective-permute-start.4 = (bf16[4,48,1536]{2,1,0:T(8,128)(2,1)S(1)}, bf16[4,48,1536]{2,1,0:T(8,128)(2,1)S(1)}, u32[]{:S(2)}, u32[]{:S(2)}) collective-permute-start(bf16[4,48,1536]{2,1,0:T(8,128)(2,1)S(1)} %pad_maximum_fusion.2.refs_0_), channel_id=1, source_target_pairs={{0,8},{1,9},{2,10},{3,11},{4,12},{5,13},{6,14},{7,15},{8,16},{9,17... | collective-permute-start | bytes 1769480 | tf_op jit(solution)/shard_map/ppermute | solution.py:62
  22.4 25.7 %collective-permute-start.9 = (bf16[4,48,1536]{2,1,0:T(8,128)(2,1)S(1)}, bf16[4,48,1536]{2,1,0:T(8,128)(2,1)S(1)}, u32[]{:S(2)}, u32[]{:S(2)}) collective-permute-start(bf16[4,48,1536]{2,1,0:T(8,128)(2,1)S(1)} %pad_maximum_fusion.2.refs_0_), channel_id=1, source_target_pairs={{0,56},{1,57},{2,58},{3,59},{4,60},{5,61},{6,62},{7,63},{8,0},{9,1... | collective-permute-start | bytes 1769480 | tf_op jit(solution)/shard_map/ppermute | solution.py:62
  25.0 24.8 %collective-permute-start.7 = (bf16[4,48,1536]{2,1,0:T(8,128)(2,1)S(1)}, bf16[4,48,1536]{2,1,0:T(8,128)(2,1)S(1)}, u32[]{:S(2)}, u32[]{:S(2)}) collective-permute-start(bf16[4,48,1536]{2,1,0:T(8,128)(2,1)S(1)} %pad_maximum_fusion.2.refs_0_), channel_id=1, source_target_pairs={{0,64},{1,65},{2,66},{3,67},{4,68},{5,69},{6,70},{7,71},{8,72},{9,... | collective-permute-start | bytes 1769480 | tf_op jit(solution)/shard_map/ppermute | solution.py:62
  28.5 10.2 %collective-permute-start.26 = (bf16[1,48,1536]{2,1,0:T(8,128)(2,1)S(1)}, bf16[1,48,1536]{2,1,0:T(8,128)(2,1)S(1)}, u32[]{:S(2)}, u32[]{:S(2)}) collective-permute-start(bf16[1,48,1536]{2,1,0:T(8,128)(2,1)S(1)} %collective-permute-done.24), channel_id=1, source_target_pairs={{0,8},{1,9},{2,10},{3,11},{4,12},{5,13},{6,14},{7,15},{8,16},{9,17... | collective-permute-start | bytes 442376 | tf_op jit(solution)/shard_map/ppermute | solution.py:62
  28.5 10.2 %collective-permute-start.27 = (bf16[1,48,1536]{2,1,0:T(8,128)(2,1)S(1)}, bf16[1,48,1536]{2,1,0:T(8,128)(2,1)S(1)}, u32[]{:S(2)}, u32[]{:S(2)}) collective-permute-start(bf16[1,48,1536]{2,1,0:T(8,128)(2,1)S(1)} %collective-permute-done.25), channel_id=1, source_target_pairs={{0,56},{1,57},{2,58},{3,59},{4,60},{5,61},{6,62},{7,63},{8,0},{9,1... | collective-permute-start | bytes 442376 | tf_op jit(solution)/shard_map/ppermute | solution.py:62
  43.9 14.8 %collective-permute-start.11 = (bf16[4,48,1536]{2,1,0:T(8,128)(2,1)S(1)}, bf16[4,48,1536]{2,1,0:T(8,128)(2,1)S(1)}, u32[]{:S(2)}, u32[]{:S(2)}) collective-permute-start(bf16[4,48,1536]{2,1,0:T(8,128)(2,1)S(1)} %collective-permute-done.4.refs_2_), channel_id=1, source_target_pairs={{0,8},{1,9},{2,10},{3,11},{4,12},{5,13},{6,14},{7,15},{8,16},{9,17... | collective-permute-start | bytes 1769480 | tf_op jit(solution)/shard_map/ppermute | solution.py:62
  44.0 34.4 %collective-permute-start.5 = (bf16[2,16,8,1536]{3,2,1,0:T(8,128)(2,1)S(1)}, bf16[2,16,8,1536]{3,2,1,0:T(8,128)(2,1)S(1)}, u32[]{:S(2)}, u32[]{:S(2)}) collective-permute-start(bf16[2,16,8,1536]{3,2,1,0:T(8,128)(2,1)S(1)} %get-tuple-element.5), channel_id=1, source_target_pairs={{0,63},{1,0},{2,1},{3,2},{4,3},{5,4},{6,5},{7,6},{8,7},{9,8},{10,9... | collective-permute-start | bytes 2359304 | tf_op jit(solution)/shard_map/ppermute | solution.py:67
  48.1 21.6 %collective-permute-start.13 = (bf16[4,48,1536]{2,1,0:T(8,128)(2,1)S(1)}, bf16[4,48,1536]{2,1,0:T(8,128)(2,1)S(1)}, u32[]{:S(2)}, u32[]{:S(2)}) collective-permute-start(bf16[4,48,1536]{2,1,0:T(8,128)(2,1)S(1)} %collective-permute-done.9.refs_4_), channel_id=1, source_target_pairs={{0,56},{1,57},{2,58},{3,59},{4,60},{5,61},{6,62},{7,63},{8,0},{9,1... | collective-permute-start | bytes 1769480 | tf_op jit(solution)/shard_map/ppermute | solution.py:62
  49.7 39.8 %collective-permute-start.32 = (bf16[8,48,1536]{2,1,0:T(8,128)(2,1)S(1)}, bf16[8,48,1536]{2,1,0:T(8,128)(2,1)S(1)}, u32[]{:S(2)}, u32[]{:S(2)}) collective-permute-start(bf16[8,48,1536]{2,1,0:T(8,128)(2,1)S(1)} %constant_dynamic-update-slice_fusion.refs_18_), channel_id=1, source_target_pairs={{0,2},{1,3},{2,4},{3,5},{4,6},{5,7},{6,0},{7,1},{8,10},{9,11},{10,... | collective-permute-start | bytes 3538952 | tf_op jit(solution)/shard_map/ppermute | solution.py:62
  49.9 39.7 %collective-permute-start.34 = (bf16[8,48,1536]{2,1,0:T(8,128)(2,1)S(1)}, bf16[8,48,1536]{2,1,0:T(8,128)(2,1)S(1)}, u32[]{:S(2)}, u32[]{:S(2)}) collective-permute-start(bf16[8,48,1536]{2,1,0:T(8,128)(2,1)S(1)} %constant_dynamic-update-slice_fusion.refs_18_), channel_id=1, source_target_pairs={{0,6},{1,7},{2,0},{3,1},{4,2},{5,3},{6,4},{7,5},{8,14},{9,15},{10,... | collective-permute-start | bytes 3538952 | tf_op jit(solution)/shard_map/ppermute | solution.py:62
  58.8 19.8 %collective-permute-start.8 = (bf16[4,48,1536]{2,1,0:T(8,128)(2,1)S(1)}, bf16[4,48,1536]{2,1,0:T(8,128)(2,1)S(1)}, u32[]{:S(2)}, u32[]{:S(2)}) collective-permute-start(bf16[4,48,1536]{2,1,0:T(8,128)(2,1)S(1)} %collective-permute-done.4.refs_2_), channel_id=1, source_target_pairs={{0,64},{1,65},{2,66},{3,67},{4,68},{5,69},{6,70},{7,71},{8,72},{9,... | collective-permute-start | bytes 1769480 | tf_op jit(solution)/shard_map/ppermute | solution.py:62
  69.7 11.3 %collective-permute-start.10 = (bf16[4,48,1536]{2,1,0:T(8,128)(2,1)S(1)}, bf16[4,48,1536]{2,1,0:T(8,128)(2,1)S(1)}, u32[]{:S(2)}, u32[]{:S(2)}) collective-permute-start(bf16[4,48,1536]{2,1,0:T(8,128)(2,1)S(1)} %collective-permute-done.9.refs_4_), channel_id=1, source_target_pairs={{0,64},{1,65},{2,66},{3,67},{4,68},{5,69},{6,70},{7,71},{8,72},{9,... | collective-permute-start | bytes 1769480 | tf_op jit(solution)/shard_map/ppermute | solution.py:62
  78.5 23.0 %collective-permute-start.31 = (bf16[8,48,1536]{2,1,0:T(8,128)(2,1)S(1)}, bf16[8,48,1536]{2,1,0:T(8,128)(2,1)S(1)}, u32[]{:S(2)}, u32[]{:S(2)}) collective-permute-start(bf16[8,48,1536]{2,1,0:T(8,128)(2,1)S(1)} %constant_dynamic-update-slice_fusion.refs_18_), channel_id=1, source_target_pairs={{0,64},{1,65},{2,66},{3,67},{4,68},{5,69},{6,70},{7,71},{8,72},{9,... | collective-permute-start | bytes 3538952 | tf_op jit(solution)/shard_map/ppermute | solution.py:62
  78.6 7.5 %collective-permute-start.6 = (bf16[2,2,16,1536]{3,2,1,0:T(8,128)(2,1)S(1)}, bf16[2,2,16,1536]{3,2,1,0:T(8,128)(2,1)S(1)}, u32[]{:S(2)}, u32[]{:S(2)}) collective-permute-start(bf16[2,2,16,1536]{3,2,1,0:T(8,128)(2,1)S(1)} %pad_maximum_fusion.3), channel_id=1, source_target_pairs={{64,0},{128,64},{192,128},{65,1},{129,65},{193,129},{66,2},{130,66... | collective-permute-start | bytes 589832 | tf_op jit(solution)/shard_map/ppermute | solution.py:72
  81.0 16.8 %collective-permute-start.15 = (bf16[4,48,1536]{2,1,0:T(8,128)(2,1)S(1)}, bf16[4,48,1536]{2,1,0:T(8,128)(2,1)}, u32[]{:S(2)}, u32[]{:S(2)}) collective-permute-start(bf16[4,48,1536]{2,1,0:T(8,128)(2,1)S(1)} %collective-permute-done.11.refs_6_), channel_id=1, source_target_pairs={{0,8},{1,9},{2,10},{3,11},{4,12},{5,13},{6,14},{7,15},{8,16},{9,17... | collective-permute-start | bytes 1769480 | tf_op jit(solution)/shard_map/ppermute | solution.py:62
  86.1 13.4 %collective-permute-start.17 = (bf16[4,48,1536]{2,1,0:T(8,128)(2,1)S(1)}, bf16[4,48,1536]{2,1,0:T(8,128)(2,1)S(1)}, u32[]{:S(2)}, u32[]{:S(2)}) collective-permute-start(bf16[4,48,1536]{2,1,0:T(8,128)(2,1)S(1)} %collective-permute-done.13.refs_8_), channel_id=1, source_target_pairs={{0,56},{1,57},{2,58},{3,59},{4,60},{5,61},{6,62},{7,63},{8,0},{9,1... | collective-permute-start | bytes 1769480 | tf_op jit(solution)/shard_map/ppermute | solution.py:62
  89.5 12.5 %collective-permute-start.12 = (bf16[4,48,1536]{2,1,0:T(8,128)(2,1)S(1)}, bf16[4,48,1536]{2,1,0:T(8,128)(2,1)S(1)}, u32[]{:S(2)}, u32[]{:S(2)}) collective-permute-start(bf16[4,48,1536]{2,1,0:T(8,128)(2,1)S(1)} %collective-permute-done.11.refs_6_), channel_id=1, source_target_pairs={{0,64},{1,65},{2,66},{3,67},{4,68},{5,69},{6,70},{7,71},{8,72},{9,... | collective-permute-start | bytes 1769480 | tf_op jit(solution)/shard_map/ppermute | solution.py:62
  89.6 14.7 %collective-permute-start.14 = (bf16[4,48,1536]{2,1,0:T(8,128)(2,1)S(1)}, bf16[4,48,1536]{2,1,0:T(8,128)(2,1)S(1)}, u32[]{:S(2)}, u32[]{:S(2)}) collective-permute-start(bf16[4,48,1536]{2,1,0:T(8,128)(2,1)S(1)} %collective-permute-done.13.refs_8_), channel_id=1, source_target_pairs={{0,64},{1,65},{2,66},{3,67},{4,68},{5,69},{6,70},{7,71},{8,72},{9,... | collective-permute-start | bytes 1769480 | tf_op jit(solution)/shard_map/ppermute | solution.py:62
  97.8 15.8 %collective-permute-start.36 = (bf16[8,48,768]{2,1,0:T(8,128)(2,1)S(1)}, bf16[8,48,768]{2,1,0:T(8,128)(2,1)}, u32[]{:S(2)}, u32[]{:S(2)}) collective-permute-start(bf16[8,48,768]{2,1,0:T(8,128)(2,1)S(1)} %slice.78), channel_id=1, source_target_pairs={{0,2},{1,3},{2,4},{3,5},{4,6},{5,7},{6,0},{7,1},{8,10},{9,11},{10,... | collective-permute-start | bytes 1769480 | tf_op jit(solution)/shard_map/ppermute | solution.py:62
  99.5 15.4 %collective-permute-start.38 = (bf16[8,48,768]{2,1,0:T(8,128)(2,1)S(1)}, bf16[8,48,768]{2,1,0:T(8,128)(2,1)}, u32[]{:S(2)}, u32[]{:S(2)}) collective-permute-start(bf16[8,48,768]{2,1,0:T(8,128)(2,1)S(1)} %slice.79), channel_id=1, source_target_pairs={{0,6},{1,7},{2,0},{3,1},{4,2},{5,3},{6,4},{7,5},{8,14},{9,15},{10,... | collective-permute-start | bytes 1769480 | tf_op jit(solution)/shard_map/ppermute | solution.py:62
  101.5 9.0 %collective-permute-start.19 = (bf16[4,48,768]{2,1,0:T(8,128)(2,1)S(1)}, bf16[4,48,768]{2,1,0:T(8,128)(2,1)}, u32[]{:S(2)}, u32[]{:S(2)}) collective-permute-start(bf16[4,48,768]{2,1,0:T(8,128)(2,1)S(1)} %slice.76), channel_id=1, source_target_pairs={{0,8},{1,9},{2,10},{3,11},{4,12},{5,13},{6,14},{7,15},{8,16},{9,17... | collective-permute-start | bytes 884744 | tf_op jit(solution)/shard_map/ppermute | solution.py:62
  102.0 10.3 %collective-permute-start.21 = (bf16[4,48,768]{2,1,0:T(8,128)(2,1)S(1)}, bf16[4,48,768]{2,1,0:T(8,128)(2,1)}, u32[]{:S(2)}, u32[]{:S(2)}) collective-permute-start(bf16[4,48,768]{2,1,0:T(8,128)(2,1)S(1)} %slice.77), channel_id=1, source_target_pairs={{0,56},{1,57},{2,58},{3,59},{4,60},{5,61},{6,62},{7,63},{8,0},{9,1... | collective-permute-start | bytes 884744 | tf_op jit(solution)/shard_map/ppermute | solution.py:62
  105.2 12.9 %collective-permute-start.16 = (bf16[4,48,1536]{2,1,0:T(8,128)(2,1)}, bf16[4,48,1536]{2,1,0:T(8,128)(2,1)}, u32[]{:S(2)}, u32[]{:S(2)}) collective-permute-start(bf16[4,48,1536]{2,1,0:T(8,128)(2,1)} %collective-permute-done.15.refs_10_), channel_id=1, source_target_pairs={{0,64},{1,65},{2,66},{3,67},{4,68},{5,69},{6,70},{7,71},{8,72},{9,... | collective-permute-start | bytes 1769480 | tf_op jit(solution)/shard_map/ppermute | solution.py:62
  110.5 12.8 %collective-permute-start.33 = (bf16[8,48,1536]{2,1,0:T(8,128)(2,1)}, bf16[8,48,1536]{2,1,0:T(8,128)(2,1)}, u32[]{:S(2)}, u32[]{:S(2)}) collective-permute-start(bf16[8,48,1536]{2,1,0:T(8,128)(2,1)} %copy-done.4), channel_id=1, source_target_pairs={{0,64},{1,65},{2,66},{3,67},{4,68},{5,69},{6,70},{7,71},{8,72},{9,... | collective-permute-start | bytes 3538952 | tf_op jit(solution)/shard_map/ppermute | solution.py:62
  112.3 11.0 %collective-permute-start.35 = (bf16[8,48,1536]{2,1,0:T(8,128)(2,1)}, bf16[8,48,1536]{2,1,0:T(8,128)(2,1)}, u32[]{:S(2)}, u32[]{:S(2)}) collective-permute-start(bf16[8,48,1536]{2,1,0:T(8,128)(2,1)} %copy-done.5), channel_id=1, source_target_pairs={{0,64},{1,65},{2,66},{3,67},{4,68},{5,69},{6,70},{7,71},{8,72},{9,... | collective-permute-start | bytes 3538952 | tf_op jit(solution)/shard_map/ppermute | solution.py:62
  156.5 25.1 %collective-permute-start.42 = (bf16[2,14,8,1536]{3,2,1,0:T(8,128)(2,1)S(1)}, bf16[2,14,8,1536]{3,2,1,0:T(8,128)(2,1)S(1)}, u32[]{:S(2)}, u32[]{:S(2)}) collective-permute-start(bf16[2,14,8,1536]{3,2,1,0:T(8,128)(2,1)S(1)} %get-tuple-element.10), channel_id=1, source_target_pairs={{0,1},{1,2},{2,3},{3,4},{4,5},{5,6},{6,7},{7,8},{8,9},{9,10},{10,1... | collective-permute-start | bytes 2064392 | tf_op jit(solution)/shard_map/ppermute | solution.py:67
  157.5 24.1 %collective-permute-start.40 = (bf16[2,2,8,1536]{3,2,1,0:T(8,128)(2,1)S(1)}, bf16[2,2,8,1536]{3,2,1,0:T(8,128)(2,1)S(1)}, u32[]{:S(2)}, u32[]{:S(2)}) collective-permute-start(bf16[2,2,8,1536]{3,2,1,0:T(8,128)(2,1)S(1)} %get-tuple-element.8), channel_id=1, source_target_pairs={{0,65},{1,66},{2,67},{3,68},{4,69},{5,70},{6,71},{7,72},{8,73},{9,... | collective-permute-start | bytes 294920 | tf_op jit(solution)/shard_map/ppermute | solution.py:62
  162.8 18.8 %collective-permute-start.41 = (bf16[2,2,8,1536]{3,2,1,0:T(8,128)(2,1)S(1)}, bf16[2,2,8,1536]{3,2,1,0:T(8,128)(2,1)S(1)}, u32[]{:S(2)}, u32[]{:S(2)}) collective-permute-start(bf16[2,2,8,1536]{3,2,1,0:T(8,128)(2,1)S(1)} %get-tuple-element.9), channel_id=1, source_target_pairs={{0,64},{64,128},{128,192},{1,65},{65,129},{129,193},{2,66},{66,130... | collective-permute-start | bytes 294920 | tf_op jit(solution)/shard_map/ppermute | solution.py:72
  (33 other events, 439.2 us)

commit v2 on v1

--- a/solution.py
+++ b/solution.py
@@ -115,7 +115,7 @@
     second = jnp.concatenate(parts)
     zs = (0, 1, -1, 2, -2, 3, -3, 4)
     found = [([(d, s) for s in Y_ORDER], c, b) for d, c, b in far_ring(first, "z", 4)]
-    early = found[1][2]
+    early = (found[1][2], found[2][2])
     found += [([(s, d) for s in zs], D + c, b) for d, c, b in far_ring(second, "y", 2)]
     plan, blocks = [], []
     for distances, column, block in found:
@@ -125,7 +125,7 @@
 
 
 def pull_ahead(tensor, early):
-    edge = lon_ring(after(tensor[:, :, :SHIFT_LON], early), -1)
+    edge = lon_ring(after(tensor[:, :, :SHIFT_LON], *early), -1)
     widened = jnp.concatenate([tensor[:, :, SHIFT_LON:], edge], axis=2)
     rim = lat_line(widened[:, :SHIFT_LAT], -1)
     return jnp.concatenate([widened[:, SHIFT_LAT:], rim], axis=1)

time: 185 us -> 185 us (level)
  no operation moved by 1% of the time
where the time goes in v2:
time: 185 us
  starting transfers between devices  72.9 us (39%)
  waiting for transfers between devices  62.7 us (34%)
  Pallas kernels  32.8 us (18%)
  local copies, waits for them, and re-layouts  9.68 us (5%)
  other arithmetic  5.78 us (3%)
    ppermute x39, starting transfers between devices, send(): return lax.ppermute(value, AXES, pairs)  64 us
    ppermute x39, waiting for transfers between devices, send(): return lax.ppermute(value, AXES, pairs)  58.6 us
    pallas_call x1, Pallas kernels, window_attention(): pl.pallas_call(functools.partial(window_kernel, plan), out_shape=jax.Shap...  30.8 us
    ppermute x2, starting transfers between devices, lat_line(): lax.ppermute(value, LAT, [(i, i + step) for i in range(size) if 0 <= i +...  4.79 us
    ppermute x2, starting transfers between devices, lon_ring(): lax.ppermute(value, LON, [(i, (i + step) % size) for i in range(size)])  4.11 us
    ppermute x2, waiting for transfers between devices, lat_line(): lax.ppermute(value, LAT, [(i, i + step) for i in range(size) if 0 <= i +...  4.04 us
  transfers between devices with their start and end apart: 43, of which 15 were waited for; matrix products, arithmetic and copies ran while one was open for 5% of the time, Pallas kernels for 0%

profile of v2, /device:TPU:1, one launch (start us, length us, event | category | flops | bytes accessed | tf_op | source)
XLA Modules:
  0.0 185.0 jit_solution(3167795227102859725)
XLA Ops:
  1.7 3.4 %collective-permute-start.23 = (bf16[24,1536]{1,0:T(8,128)(2,1)S(1)}, bf16[24,1536]{1,0:T(8,128)(2,1)S(1)}, u32[]{:S(2)}, u32[]{:S(2)}) collective-permute-start(bf16[24,1536]{1,0:T(8,128)(2,1)S(1)} %get-tuple-element.16), channel_id=1, source_target_pairs={{0,129},{1,128},{2,131},{3,130},{4,133},{5,132},{6,135},{7,134},{8... | collective-permute-start | bytes 221192 | tf_op jit(solution)/shard_map/ppermute | solution.py:62
  6.8 1.9 %collective-permute-start.24 = (bf16[1,48,1536]{2,1,0:T(8,128)(2,1)S(1)}, bf16[1,48,1536]{2,1,0:T(8,128)(2,1)S(1)}, u32[]{:S(2)}, u32[]{:S(2)}) collective-permute-start(bf16[1,48,1536]{2,1,0:T(8,128)(2,1)S(1)} %maximum_bitcast_fusion.1), channel_id=1, source_target_pairs={{0,8},{1,9},{2,10},{3,11},{4,12},{5,13},{6,14},{7,15},{8,16},{9,17... | collective-permute-start | bytes 442376 | tf_op jit(solution)/shard_map/ppermute | solution.py:62
  8.7 4.0 %collective-permute-start.25 = (bf16[1,48,1536]{2,1,0:T(8,128)(2,1)S(1)}, bf16[1,48,1536]{2,1,0:T(8,128)(2,1)S(1)}, u32[]{:S(2)}, u32[]{:S(2)}) collective-permute-start(bf16[1,48,1536]{2,1,0:T(8,128)(2,1)S(1)} %maximum_bitcast_fusion.1), channel_id=1, source_target_pairs={{0,56},{1,57},{2,58},{3,59},{4,60},{5,61},{6,62},{7,63},{8,0},{9,1... | collective-permute-start | bytes 442376 | tf_op jit(solution)/shard_map/ppermute | solution.py:62
  14.2 1.5 collective-permute-start.2
  15.7 1.6 collective-permute-start.3
  18.2 4.0 %collective-permute-done.3 = bf16[1,48,1536]{2,1,0:T(8,128)(2,1)S(1)} collective-permute-done((bf16[1,48,1536]{2,1,0:T(8,128)(2,1)S(1)}, bf16[1,48,1536]{2,1,0:T(8,128)(2,1)S(1)}, u32[]{:S(2)}, u32[]{:S(2)}) %collective-permute-start.3) | collective-permute-done | bytes 147488 | tf_op jit(solution)/shard_map/ppermute | solution.py:62
  22.4 2.7 %collective-permute-start.5 = (bf16[4,48,1536]{2,1,0:T(8,128)(2,1)S(1)}, bf16[4,48,1536]{2,1,0:T(8,128)(2,1)S(1)}, u32[]{:S(2)}, u32[]{:S(2)}) collective-permute-start(bf16[4,48,1536]{2,1,0:T(8,128)(2,1)S(1)} %pad_maximum_fusion.2.refs_0_), channel_id=1, source_target_pairs={{0,56},{1,57},{2,58},{3,59},{4,60},{5,61},{6,62},{7,63},{8,0},{9,1... | collective-permute-start | bytes 1769480 | tf_op jit(solution)/shard_map/ppermute | solution.py:62
  25.0 3.4 %collective-permute-start.8 = (bf16[4,48,1536]{2,1,0:T(8,128)(2,1)S(1)}, bf16[4,48,1536]{2,1,0:T(8,128)(2,1)S(1)}, u32[]{:S(2)}, u32[]{:S(2)}) collective-permute-start(bf16[4,48,1536]{2,1,0:T(8,128)(2,1)S(1)} %pad_maximum_fusion.2.refs_0_), channel_id=1, source_target_pairs={{0,64},{1,65},{2,66},{3,67},{4,68},{5,69},{6,70},{7,71},{8,72},{9,... | collective-permute-start | bytes 1769480 | tf_op jit(solution)/shard_map/ppermute | solution.py:62
  28.5 2.7 %collective-permute-start.27 = (bf16[1,48,1536]{2,1,0:T(8,128)(2,1)S(1)}, bf16[1,48,1536]{2,1,0:T(8,128)(2,1)S(1)}, u32[]{:S(2)}, u32[]{:S(2)}) collective-permute-start(bf16[1,48,1536]{2,1,0:T(8,128)(2,1)S(1)} %collective-permute-done.25), channel_id=1, source_target_pairs={{0,56},{1,57},{2,58},{3,59},{4,60},{5,61},{6,62},{7,63},{8,0},{9,1... | collective-permute-start | bytes 442376 | tf_op jit(solution)/shard_map/ppermute | solution.py:62
  31.3 7.4 %collective-permute-done.26 = bf16[1,48,1536]{2,1,0:T(8,128)(2,1)S(1)} collective-permute-done((bf16[1,48,1536]{2,1,0:T(8,128)(2,1)S(1)}, bf16[1,48,1536]{2,1,0:T(8,128)(2,1)S(1)}, u32[]{:S(2)}, u32[]{:S(2)}) %collective-permute-start.26) | collective-permute-done | bytes 147488 | tf_op jit(solution)/shard_map/ppermute | solution.py:62
  38.7 2.7 %collective-permute-start.29 = (bf16[1,48,1536]{2,1,0:T(8,128)(2,1)S(1)}, bf16[1,48,1536]{2,1,0:T(8,128)(2,1)S(1)}, u32[]{:S(2)}, u32[]{:S(2)}) collective-permute-start(bf16[1,48,1536]{2,1,0:T(8,128)(2,1)S(1)} %collective-permute-done.27), channel_id=1, source_target_pairs={{0,56},{1,57},{2,58},{3,59},{4,60},{5,61},{6,62},{7,63},{8,0},{9,1... | collective-permute-start | bytes 442376 | tf_op jit(solution)/shard_map/ppermute | solution.py:62
  41.4 2.5 %collective-permute-done.28 = bf16[1,48,1536]{2,1,0:T(8,128)(2,1)S(1)} collective-permute-done((bf16[1,48,1536]{2,1,0:T(8,128)(2,1)S(1)}, bf16[1,48,1536]{2,1,0:T(8,128)(2,1)S(1)}, u32[]{:S(2)}, u32[]{:S(2)}) %collective-permute-start.28) | collective-permute-done | bytes 147488 | tf_op jit(solution)/shard_map/ppermute | solution.py:62
  44.1 4.0 %collective-permute-start.6 = (bf16[2,16,8,1536]{3,2,1,0:T(8,128)(2,1)S(1)}, bf16[2,16,8,1536]{3,2,1,0:T(8,128)(2,1)S(1)}, u32[]{:S(2)}, u32[]{:S(2)}) collective-permute-start(bf16[2,16,8,1536]{3,2,1,0:T(8,128)(2,1)S(1)} %get-tuple-element.5), channel_id=1, source_target_pairs={{0,63},{1,0},{2,1},{3,2},{4,3},{5,4},{6,5},{7,6},{8,7},{9,8},{10,9... | collective-permute-start | bytes 2359304 | tf_op jit(solution)/shard_map/ppermute | solution.py:67
  49.9 2.6 %collective-permute-start.34 = (bf16[8,48,1536]{2,1,0:T(8,128)(2,1)S(1)}, bf16[8,48,1536]{2,1,0:T(8,128)(2,1)S(1)}, u32[]{:S(2)}, u32[]{:S(2)}) collective-permute-start(bf16[8,48,1536]{2,1,0:T(8,128)(2,1)S(1)} %constant_dynamic-update-slice_fusion.refs_18_), channel_id=1, source_target_pairs={{0,6},{1,7},{2,0},{3,1},{4,2},{5,3},{6,4},{7,5},{8,14},{9,15},{10,... | collective-permute-start | bytes 3538952 | tf_op jit(solution)/shard_map/ppermute | solution.py:62
  52.5 6.2 %collective-permute-done.11.refs_6_ = bf16[4,48,1536]{2,1,0:T(8,128)(2,1)S(1)} collective-permute-done((bf16[4,48,1536]{2,1,0:T(8,128)(2,1)S(1)}, bf16[4,48,1536]{2,1,0:T(8,128)(2,1)S(1)}, u32[]{:S(2)}, u32[]{:S(2)}) %collective-permute-start.11) | collective-permute-done | bytes 589856 | tf_op jit(solution)/shard_map/ppermute | solution.py:62
  58.8 5.9 %collective-permute-start.10 = (bf16[4,48,1536]{2,1,0:T(8,128)(2,1)S(1)}, bf16[4,48,1536]{2,1,0:T(8,128)(2,1)S(1)}, u32[]{:S(2)}, u32[]{:S(2)}) collective-permute-start(bf16[4,48,1536]{2,1,0:T(8,128)(2,1)S(1)} %collective-permute-done.5.refs_4_), channel_id=1, source_target_pairs={{0,64},{1,65},{2,66},{3,67},{4,68},{5,69},{6,70},{7,71},{8,72},{9,... | collective-permute-start | bytes 1769480 | tf_op jit(solution)/shard_map/ppermute | solution.py:62
  64.6 5.1 %collective-permute-done.13.refs_8_ = bf16[4,48,1536]{2,1,0:T(8,128)(2,1)S(1)} collective-permute-done((bf16[4,48,1536]{2,1,0:T(8,128)(2,1)S(1)}, bf16[4,48,1536]{2,1,0:T(8,128)(2,1)S(1)}, u32[]{:S(2)}, u32[]{:S(2)}) %collective-permute-start.13) | collective-permute-done | bytes 589856 | tf_op jit(solution)/shard_map/ppermute | solution.py:62
  69.7 8.8 %collective-permute-start.9 = (bf16[4,48,1536]{2,1,0:T(8,128)(2,1)S(1)}, bf16[4,48,1536]{2,1,0:T(8,128)(2,1)S(1)}, u32[]{:S(2)}, u32[]{:S(2)}) collective-permute-start(bf16[4,48,1536]{2,1,0:T(8,128)(2,1)S(1)} %collective-permute-done.4.refs_2_), channel_id=1, source_target_pairs={{0,64},{1,65},{2,66},{3,67},{4,68},{5,69},{6,70},{7,71},{8,72},{9,... | collective-permute-start | bytes 1769480 | tf_op jit(solution)/shard_map/ppermute | solution.py:62
  78.6 2.3 %collective-permute-start.7 = (bf16[2,2,16,1536]{3,2,1,0:T(8,128)(2,1)S(1)}, bf16[2,2,16,1536]{3,2,1,0:T(8,128)(2,1)S(1)}, u32[]{:S(2)}, u32[]{:S(2)}) collective-permute-start(bf16[2,2,16,1536]{3,2,1,0:T(8,128)(2,1)S(1)} %pad_maximum_fusion.3), channel_id=1, source_target_pairs={{64,0},{128,64},{192,128},{65,1},{129,65},{193,129},{66,2},{130,66... | collective-permute-start | bytes 589832 | tf_op jit(solution)/shard_map/ppermute | solution.py:72
  82.1 4.0 %collective-permute-done.7 = bf16[2,2,16,1536]{3,2,1,0:T(8,128)(2,1)S(1)} collective-permute-done((bf16[2,2,16,1536]{3,2,1,0:T(8,128)(2,1)S(1)}, bf16[2,2,16,1536]{3,2,1,0:T(8,128)(2,1)S(1)}, u32[]{:S(2)}, u32[]{:S(2)}) %collective-permute-start.7) | collective-permute-done | bytes 196640 | tf_op jit(solution)/shard_map/ppermute | solution.py:72
  86.1 3.4 %collective-permute-start.17 = (bf16[4,48,1536]{2,1,0:T(8,128)(2,1)S(1)}, bf16[4,48,1536]{2,1,0:T(8,128)(2,1)S(1)}, u32[]{:S(2)}, u32[]{:S(2)}) collective-permute-start(bf16[4,48,1536]{2,1,0:T(8,128)(2,1)S(1)} %collective-permute-done.13.refs_8_), channel_id=1, source_target_pairs={{0,56},{1,57},{2,58},{3,59},{4,60},{5,61},{6,62},{7,63},{8,0},{9,1... | collective-permute-start | bytes 1769480 | tf_op jit(solution)/shard_map/ppermute | solution.py:62
  90.3 7.5 %collective-permute-done.15.refs_10_ = bf16[4,48,1536]{2,1,0:T(8,128)(2,1)} collective-permute-done((bf16[4,48,1536]{2,1,0:T(8,128)(2,1)S(1)}, bf16[4,48,1536]{2,1,0:T(8,128)(2,1)}, u32[]{:S(2)}, u32[]{:S(2)}) %collective-permute-start.15) | collective-permute-done | bytes 589856 | tf_op jit(solution)/shard_map/ppermute | solution.py:62
  97.8 1.7 collective-permute-done.17.refs_12_
  102.0 2.3 %collective-permute-start.21 = (bf16[4,48,768]{2,1,0:T(8,128)(2,1)S(1)}, bf16[4,48,768]{2,1,0:T(8,128)(2,1)}, u32[]{:S(2)}, u32[]{:S(2)}) collective-permute-start(bf16[4,48,768]{2,1,0:T(8,128)(2,1)S(1)} %slice.77), channel_id=1, source_target_pairs={{0,56},{1,57},{2,58},{3,59},{4,60},{5,61},{6,62},{7,63},{8,0},{9,1... | collective-permute-start | bytes 884744 | tf_op jit(solution)/shard_map/ppermute | solution.py:62
  106.8 3.6 %collective-permute-done.19.refs_14_ = bf16[4,48,768]{2,1,0:T(8,128)(2,1)} collective-permute-done((bf16[4,48,768]{2,1,0:T(8,128)(2,1)S(1)}, bf16[4,48,768]{2,1,0:T(8,128)(2,1)}, u32[]{:S(2)}, u32[]{:S(2)}) %collective-permute-start.19) | collective-permute-done | bytes 294944 | tf_op jit(solution)/shard_map/ppermute | solution.py:62
  110.5 1.9 %collective-permute-start.33 = (bf16[8,48,1536]{2,1,0:T(8,128)(2,1)}, bf16[8,48,1536]{2,1,0:T(8,128)(2,1)}, u32[]{:S(2)}, u32[]{:S(2)}) collective-permute-start(bf16[8,48,1536]{2,1,0:T(8,128)(2,1)} %copy-done.4), channel_id=1, source_target_pairs={{0,64},{1,65},{2,66},{3,67},{4,68},{5,69},{6,70},{7,71},{8,72},{9,... | collective-permute-start | bytes 3538952 | tf_op jit(solution)/shard_map/ppermute | solution.py:62
  115.8 1.8 collective-permute-done.20.refs_15_
  124.3 30.8 %window_attention.1 = bf16[2,256,1536]{2,1,0:T(8,128)(2,1)} custom-call(s32[3]{0:T(128)} %pad_add_fusion.pos, bf16[256,1536]{1,0:T(8,128)(2,1)} %bitcast.33, bf16[256,1536]{1,0:T(8,128)(2,1)} %bitcast.32, f32[256,128]{1,0:T(8,128)} %add_convert_fusion.mask, f32[1,1536]{1,0:T(1,128)} %broadcast_in_dim.18.gain, f32[12,128]{1,0:T(8,128)} %broadcast_in_dim.21.scale, ...), custom_call_target="tpu_custom_call" | custom-call | flops 11000000512 | bytes 24000000 | tf_op jit(solution)/shard_map/window_attention/pallas_call | solution.py:289
  157.6 5.2 %collective-permute-start.40 = (bf16[2,2,8,1536]{3,2,1,0:T(8,128)(2,1)S(1)}, bf16[2,2,8,1536]{3,2,1,0:T(8,128)(2,1)S(1)}, u32[]{:S(2)}, u32[]{:S(2)}) collective-permute-start(bf16[2,2,8,1536]{3,2,1,0:T(8,128)(2,1)S(1)} %get-tuple-element.8), channel_id=1, source_target_pairs={{0,65},{1,66},{2,67},{3,68},{4,69},{5,70},{6,71},{7,72},{8,73},{9,... | collective-permute-start | bytes 294920 | tf_op jit(solution)/shard_map/ppermute | solution.py:62
  162.8 2.5 %collective-permute-start.41 = (bf16[2,2,8,1536]{3,2,1,0:T(8,128)(2,1)S(1)}, bf16[2,2,8,1536]{3,2,1,0:T(8,128)(2,1)S(1)}, u32[]{:S(2)}, u32[]{:S(2)}) collective-permute-start(bf16[2,2,8,1536]{3,2,1,0:T(8,128)(2,1)S(1)} %get-tuple-element.9), channel_id=1, source_target_pairs={{0,64},{64,128},{128,192},{1,65},{65,129},{129,193},{2,66},{66,130... | collective-permute-start | bytes 294920 | tf_op jit(solution)/shard_map/ppermute | solution.py:72
  165.2 16.4 %collective-permute-done.40 = bf16[2,2,8,1536]{3,2,1,0:T(8,128)(2,1)S(1)} collective-permute-done((bf16[2,2,8,1536]{3,2,1,0:T(8,128)(2,1)S(1)}, bf16[2,2,8,1536]{3,2,1,0:T(8,128)(2,1)S(1)}, u32[]{:S(2)}, u32[]{:S(2)}) %collective-permute-start.40) | collective-permute-done | bytes 98336 | tf_op jit(solution)/shard_map/ppermute | solution.py:62
  183.0 2.0 %finish.1 = (bf16[256,1536]{1,0:T(8,128)(2,1)}, bf16[256,1536]{1,0:T(8,128)(2,1)}) custom-call(bf16[256,1536]{1,0:T(8,128)(2,1)S(1)} %bitcast.27, bf16[256,1536]{1,0:T(8,128)(2,1)S(1)} %bitcast.29, bf16[2,256,1536]{2,1,0:T(8,128)(2,1)S(1)} %bitcast.25, f32[1,1536]{1,0:T(1,128)S(1)} %copy-done.2), custom_call_target="tpu_custom_call" | custom-call | tf_op jit(solution)/shard_map/finish/pallas_call | solution.py:328
  (139 shorter events, 27.9 us)
Async XLA Ops:
  5.1 7.7 %collective-permute-start = (bf16[24,1536]{1,0:T(8,128)(2,1)S(1)}, bf16[24,1536]{1,0:T(8,128)(2,1)S(1)}, u32[]{:S(2)}, u32[]{:S(2)}) collective-permute-start(bf16[24,1536]{1,0:T(8,128)(2,1)S(1)} %get-tuple-element.17), channel_id=1, source_target_pairs={{0,129},{1,128},{2,131},{3,130},{4,133},{5,132},{6,135},{7,134},{8... | collective-permute-start | bytes 221192 | tf_op jit(solution)/shard_map/ppermute | solution.py:62
  6.8 21.6 %collective-permute-start.24 = (bf16[1,48,1536]{2,1,0:T(8,128)(2,1)S(1)}, bf16[1,48,1536]{2,1,0:T(8,128)(2,1)S(1)}, u32[]{:S(2)}, u32[]{:S(2)}) collective-permute-start(bf16[1,48,1536]{2,1,0:T(8,128)(2,1)S(1)} %maximum_bitcast_fusion.1), channel_id=1, source_target_pairs={{0,8},{1,9},{2,10},{3,11},{4,12},{5,13},{6,14},{7,15},{8,16},{9,17... | collective-permute-start | bytes 442376 | tf_op jit(solution)/shard_map/ppermute | solution.py:62
  8.7 19.8 %collective-permute-start.25 = (bf16[1,48,1536]{2,1,0:T(8,128)(2,1)S(1)}, bf16[1,48,1536]{2,1,0:T(8,128)(2,1)S(1)}, u32[]{:S(2)}, u32[]{:S(2)}) collective-permute-start(bf16[1,48,1536]{2,1,0:T(8,128)(2,1)S(1)} %maximum_bitcast_fusion.1), channel_id=1, source_target_pairs={{0,56},{1,57},{2,58},{3,59},{4,60},{5,61},{6,62},{7,63},{8,0},{9,1... | collective-permute-start | bytes 442376 | tf_op jit(solution)/shard_map/ppermute | solution.py:62
  15.7 6.5 %collective-permute-start.3 = (bf16[1,48,1536]{2,1,0:T(8,128)(2,1)S(1)}, bf16[1,48,1536]{2,1,0:T(8,128)(2,1)S(1)}, u32[]{:S(2)}, u32[]{:S(2)}) collective-permute-start(bf16[1,48,1536]{2,1,0:T(8,128)(2,1)S(1)} %maximum_bitcast_fusion), channel_id=1, source_target_pairs={{0,4},{1,5},{2,6},{3,7},{4,0},{5,1},{6,2},{7,3},{8,12},{9,13},{10,... | collective-permute-start | bytes 442376 | tf_op jit(solution)/shard_map/ppermute | solution.py:62
  22.3 21.6 %collective-permute-start.4 = (bf16[4,48,1536]{2,1,0:T(8,128)(2,1)S(1)}, bf16[4,48,1536]{2,1,0:T(8,128)(2,1)S(1)}, u32[]{:S(2)}, u32[]{:S(2)}) collective-permute-start(bf16[4,48,1536]{2,1,0:T(8,128)(2,1)S(1)} %pad_maximum_fusion.2.refs_0_), channel_id=1, source_target_pairs={{0,8},{1,9},{2,10},{3,11},{4,12},{5,13},{6,14},{7,15},{8,16},{9,17... | collective-permute-start | bytes 1769480 | tf_op jit(solution)/shard_map/ppermute | solution.py:62
  22.4 21.7 %collective-permute-start.5 = (bf16[4,48,1536]{2,1,0:T(8,128)(2,1)S(1)}, bf16[4,48,1536]{2,1,0:T(8,128)(2,1)S(1)}, u32[]{:S(2)}, u32[]{:S(2)}) collective-permute-start(bf16[4,48,1536]{2,1,0:T(8,128)(2,1)S(1)} %pad_maximum_fusion.2.refs_0_), channel_id=1, source_target_pairs={{0,56},{1,57},{2,58},{3,59},{4,60},{5,61},{6,62},{7,63},{8,0},{9,1... | collective-permute-start | bytes 1769480 | tf_op jit(solution)/shard_map/ppermute | solution.py:62
  25.0 24.8 %collective-permute-start.8 = (bf16[4,48,1536]{2,1,0:T(8,128)(2,1)S(1)}, bf16[4,48,1536]{2,1,0:T(8,128)(2,1)S(1)}, u32[]{:S(2)}, u32[]{:S(2)}) collective-permute-start(bf16[4,48,1536]{2,1,0:T(8,128)(2,1)S(1)} %pad_maximum_fusion.2.refs_0_), channel_id=1, source_target_pairs={{0,64},{1,65},{2,66},{3,67},{4,68},{5,69},{6,70},{7,71},{8,72},{9,... | collective-permute-start | bytes 1769480 | tf_op jit(solution)/shard_map/ppermute | solution.py:62
  28.5 10.2 %collective-permute-start.26 = (bf16[1,48,1536]{2,1,0:T(8,128)(2,1)S(1)}, bf16[1,48,1536]{2,1,0:T(8,128)(2,1)S(1)}, u32[]{:S(2)}, u32[]{:S(2)}) collective-permute-start(bf16[1,48,1536]{2,1,0:T(8,128)(2,1)S(1)} %collective-permute-done.24), channel_id=1, source_target_pairs={{0,8},{1,9},{2,10},{3,11},{4,12},{5,13},{6,14},{7,15},{8,16},{9,17... | collective-permute-start | bytes 442376 | tf_op jit(solution)/shard_map/ppermute | solution.py:62
  28.5 10.2 %collective-permute-start.27 = (bf16[1,48,1536]{2,1,0:T(8,128)(2,1)S(1)}, bf16[1,48,1536]{2,1,0:T(8,128)(2,1)S(1)}, u32[]{:S(2)}, u32[]{:S(2)}) collective-permute-start(bf16[1,48,1536]{2,1,0:T(8,128)(2,1)S(1)} %collective-permute-done.25), channel_id=1, source_target_pairs={{0,56},{1,57},{2,58},{3,59},{4,60},{5,61},{6,62},{7,63},{8,0},{9,1... | collective-permute-start | bytes 442376 | tf_op jit(solution)/shard_map/ppermute | solution.py:62
  43.9 14.8 %collective-permute-start.11 = (bf16[4,48,1536]{2,1,0:T(8,128)(2,1)S(1)}, bf16[4,48,1536]{2,1,0:T(8,128)(2,1)S(1)}, u32[]{:S(2)}, u32[]{:S(2)}) collective-permute-start(bf16[4,48,1536]{2,1,0:T(8,128)(2,1)S(1)} %collective-permute-done.4.refs_2_), channel_id=1, source_target_pairs={{0,8},{1,9},{2,10},{3,11},{4,12},{5,13},{6,14},{7,15},{8,16},{9,17... | collective-permute-start | bytes 1769480 | tf_op jit(solution)/shard_map/ppermute | solution.py:62
  44.1 34.4 %collective-permute-start.6 = (bf16[2,16,8,1536]{3,2,1,0:T(8,128)(2,1)S(1)}, bf16[2,16,8,1536]{3,2,1,0:T(8,128)(2,1)S(1)}, u32[]{:S(2)}, u32[]{:S(2)}) collective-permute-start(bf16[2,16,8,1536]{3,2,1,0:T(8,128)(2,1)S(1)} %get-tuple-element.5), channel_id=1, source_target_pairs={{0,63},{1,0},{2,1},{3,2},{4,3},{5,4},{6,5},{7,6},{8,7},{9,8},{10,9... | collective-permute-start | bytes 2359304 | tf_op jit(solution)/shard_map/ppermute | solution.py:67
  48.1 21.6 %collective-permute-start.13 = (bf16[4,48,1536]{2,1,0:T(8,128)(2,1)S(1)}, bf16[4,48,1536]{2,1,0:T(8,128)(2,1)S(1)}, u32[]{:S(2)}, u32[]{:S(2)}) collective-permute-start(bf16[4,48,1536]{2,1,0:T(8,128)(2,1)S(1)} %collective-permute-done.5.refs_4_), channel_id=1, source_target_pairs={{0,56},{1,57},{2,58},{3,59},{4,60},{5,61},{6,62},{7,63},{8,0},{9,1... | collective-permute-start | bytes 1769480 | tf_op jit(solution)/shard_map/ppermute | solution.py:62
  49.7 39.8 %collective-permute-start.32 = (bf16[8,48,1536]{2,1,0:T(8,128)(2,1)S(1)}, bf16[8,48,1536]{2,1,0:T(8,128)(2,1)S(1)}, u32[]{:S(2)}, u32[]{:S(2)}) collective-permute-start(bf16[8,48,1536]{2,1,0:T(8,128)(2,1)S(1)} %constant_dynamic-update-slice_fusion.refs_18_), channel_id=1, source_target_pairs={{0,2},{1,3},{2,4},{3,5},{4,6},{5,7},{6,0},{7,1},{8,10},{9,11},{10,... | collective-permute-start | bytes 3538952 | tf_op jit(solution)/shard_map/ppermute | solution.py:62
  49.9 39.7 %collective-permute-start.34 = (bf16[8,48,1536]{2,1,0:T(8,128)(2,1)S(1)}, bf16[8,48,1536]{2,1,0:T(8,128)(2,1)S(1)}, u32[]{:S(2)}, u32[]{:S(2)}) collective-permute-start(bf16[8,48,1536]{2,1,0:T(8,128)(2,1)S(1)} %constant_dynamic-update-slice_fusion.refs_18_), channel_id=1, source_target_pairs={{0,6},{1,7},{2,0},{3,1},{4,2},{5,3},{6,4},{7,5},{8,14},{9,15},{10,... | collective-permute-start | bytes 3538952 | tf_op jit(solution)/shard_map/ppermute | solution.py:62
  58.8 19.9 %collective-permute-start.10 = (bf16[4,48,1536]{2,1,0:T(8,128)(2,1)S(1)}, bf16[4,48,1536]{2,1,0:T(8,128)(2,1)S(1)}, u32[]{:S(2)}, u32[]{:S(2)}) collective-permute-start(bf16[4,48,1536]{2,1,0:T(8,128)(2,1)S(1)} %collective-permute-done.5.refs_4_), channel_id=1, source_target_pairs={{0,64},{1,65},{2,66},{3,67},{4,68},{5,69},{6,70},{7,71},{8,72},{9,... | collective-permute-start | bytes 1769480 | tf_op jit(solution)/shard_map/ppermute | solution.py:62
  69.7 11.3 %collective-permute-start.9 = (bf16[4,48,1536]{2,1,0:T(8,128)(2,1)S(1)}, bf16[4,48,1536]{2,1,0:T(8,128)(2,1)S(1)}, u32[]{:S(2)}, u32[]{:S(2)}) collective-permute-start(bf16[4,48,1536]{2,1,0:T(8,128)(2,1)S(1)} %collective-permute-done.4.refs_2_), channel_id=1, source_target_pairs={{0,64},{1,65},{2,66},{3,67},{4,68},{5,69},{6,70},{7,71},{8,72},{9,... | collective-permute-start | bytes 1769480 | tf_op jit(solution)/shard_map/ppermute | solution.py:62
  78.5 23.0 %collective-permute-start.31 = (bf16[8,48,1536]{2,1,0:T(8,128)(2,1)S(1)}, bf16[8,48,1536]{2,1,0:T(8,128)(2,1)S(1)}, u32[]{:S(2)}, u32[]{:S(2)}) collective-permute-start(bf16[8,48,1536]{2,1,0:T(8,128)(2,1)S(1)} %constant_dynamic-update-slice_fusion.refs_18_), channel_id=1, source_target_pairs={{0,64},{1,65},{2,66},{3,67},{4,68},{5,69},{6,70},{7,71},{8,72},{9,... | collective-permute-start | bytes 3538952 | tf_op jit(solution)/shard_map/ppermute | solution.py:62
  78.6 7.5 %collective-permute-start.7 = (bf16[2,2,16,1536]{3,2,1,0:T(8,128)(2,1)S(1)}, bf16[2,2,16,1536]{3,2,1,0:T(8,128)(2,1)S(1)}, u32[]{:S(2)}, u32[]{:S(2)}) collective-permute-start(bf16[2,2,16,1536]{3,2,1,0:T(8,128)(2,1)S(1)} %pad_maximum_fusion.3), channel_id=1, source_target_pairs={{64,0},{128,64},{192,128},{65,1},{129,65},{193,129},{66,2},{130,66... | collective-permute-start | bytes 589832 | tf_op jit(solution)/shard_map/ppermute | solution.py:72
  81.0 16.8 %collective-permute-start.15 = (bf16[4,48,1536]{2,1,0:T(8,128)(2,1)S(1)}, bf16[4,48,1536]{2,1,0:T(8,128)(2,1)}, u32[]{:S(2)}, u32[]{:S(2)}) collective-permute-start(bf16[4,48,1536]{2,1,0:T(8,128)(2,1)S(1)} %collective-permute-done.11.refs_6_), channel_id=1, source_target_pairs={{0,8},{1,9},{2,10},{3,11},{4,12},{5,13},{6,14},{7,15},{8,16},{9,17... | collective-permute-start | bytes 1769480 | tf_op jit(solution)/shard_map/ppermute | solution.py:62
  86.1 13.4 %collective-permute-start.17 = (bf16[4,48,1536]{2,1,0:T(8,128)(2,1)S(1)}, bf16[4,48,1536]{2,1,0:T(8,128)(2,1)S(1)}, u32[]{:S(2)}, u32[]{:S(2)}) collective-permute-start(bf16[4,48,1536]{2,1,0:T(8,128)(2,1)S(1)} %collective-permute-done.13.refs_8_), channel_id=1, source_target_pairs={{0,56},{1,57},{2,58},{3,59},{4,60},{5,61},{6,62},{7,63},{8,0},{9,1... | collective-permute-start | bytes 1769480 | tf_op jit(solution)/shard_map/ppermute | solution.py:62
  89.5 12.5 %collective-permute-start.12 = (bf16[4,48,1536]{2,1,0:T(8,128)(2,1)S(1)}, bf16[4,48,1536]{2,1,0:T(8,128)(2,1)S(1)}, u32[]{:S(2)}, u32[]{:S(2)}) collective-permute-start(bf16[4,48,1536]{2,1,0:T(8,128)(2,1)S(1)} %collective-permute-done.11.refs_6_), channel_id=1, source_target_pairs={{0,64},{1,65},{2,66},{3,67},{4,68},{5,69},{6,70},{7,71},{8,72},{9,... | collective-permute-start | bytes 1769480 | tf_op jit(solution)/shard_map/ppermute | solution.py:62
  89.6 14.7 %collective-permute-start.14 = (bf16[4,48,1536]{2,1,0:T(8,128)(2,1)S(1)}, bf16[4,48,1536]{2,1,0:T(8,128)(2,1)S(1)}, u32[]{:S(2)}, u32[]{:S(2)}) collective-permute-start(bf16[4,48,1536]{2,1,0:T(8,128)(2,1)S(1)} %collective-permute-done.13.refs_8_), channel_id=1, source_target_pairs={{0,64},{1,65},{2,66},{3,67},{4,68},{5,69},{6,70},{7,71},{8,72},{9,... | collective-permute-start | bytes 1769480 | tf_op jit(solution)/shard_map/ppermute | solution.py:62
  97.8 15.8 %collective-permute-start.36 = (bf16[8,48,768]{2,1,0:T(8,128)(2,1)S(1)}, bf16[8,48,768]{2,1,0:T(8,128)(2,1)}, u32[]{:S(2)}, u32[]{:S(2)}) collective-permute-start(bf16[8,48,768]{2,1,0:T(8,128)(2,1)S(1)} %slice.78), channel_id=1, source_target_pairs={{0,2},{1,3},{2,4},{3,5},{4,6},{5,7},{6,0},{7,1},{8,10},{9,11},{10,... | collective-permute-start | bytes 1769480 | tf_op jit(solution)/shard_map/ppermute | solution.py:62
  99.5 15.4 %collective-permute-start.38 = (bf16[8,48,768]{2,1,0:T(8,128)(2,1)S(1)}, bf16[8,48,768]{2,1,0:T(8,128)(2,1)}, u32[]{:S(2)}, u32[]{:S(2)}) collective-permute-start(bf16[8,48,768]{2,1,0:T(8,128)(2,1)S(1)} %slice.79), channel_id=1, source_target_pairs={{0,6},{1,7},{2,0},{3,1},{4,2},{5,3},{6,4},{7,5},{8,14},{9,15},{10,... | collective-permute-start | bytes 1769480 | tf_op jit(solution)/shard_map/ppermute | solution.py:62
  101.5 9.0 %collective-permute-start.19 = (bf16[4,48,768]{2,1,0:T(8,128)(2,1)S(1)}, bf16[4,48,768]{2,1,0:T(8,128)(2,1)}, u32[]{:S(2)}, u32[]{:S(2)}) collective-permute-start(bf16[4,48,768]{2,1,0:T(8,128)(2,1)S(1)} %slice.76), channel_id=1, source_target_pairs={{0,8},{1,9},{2,10},{3,11},{4,12},{5,13},{6,14},{7,15},{8,16},{9,17... | collective-permute-start | bytes 884744 | tf_op jit(solution)/shard_map/ppermute | solution.py:62
  102.0 10.3 %collective-permute-start.21 = (bf16[4,48,768]{2,1,0:T(8,128)(2,1)S(1)}, bf16[4,48,768]{2,1,0:T(8,128)(2,1)}, u32[]{:S(2)}, u32[]{:S(2)}) collective-permute-start(bf16[4,48,768]{2,1,0:T(8,128)(2,1)S(1)} %slice.77), channel_id=1, source_target_pairs={{0,56},{1,57},{2,58},{3,59},{4,60},{5,61},{6,62},{7,63},{8,0},{9,1... | collective-permute-start | bytes 884744 | tf_op jit(solution)/shard_map/ppermute | solution.py:62
  105.2 12.9 %collective-permute-start.16 = (bf16[4,48,1536]{2,1,0:T(8,128)(2,1)}, bf16[4,48,1536]{2,1,0:T(8,128)(2,1)}, u32[]{:S(2)}, u32[]{:S(2)}) collective-permute-start(bf16[4,48,1536]{2,1,0:T(8,128)(2,1)} %collective-permute-done.15.refs_10_), channel_id=1, source_target_pairs={{0,64},{1,65},{2,66},{3,67},{4,68},{5,69},{6,70},{7,71},{8,72},{9,... | collective-permute-start | bytes 1769480 | tf_op jit(solution)/shard_map/ppermute | solution.py:62
  110.5 12.8 %collective-permute-start.33 = (bf16[8,48,1536]{2,1,0:T(8,128)(2,1)}, bf16[8,48,1536]{2,1,0:T(8,128)(2,1)}, u32[]{:S(2)}, u32[]{:S(2)}) collective-permute-start(bf16[8,48,1536]{2,1,0:T(8,128)(2,1)} %copy-done.4), channel_id=1, source_target_pairs={{0,64},{1,65},{2,66},{3,67},{4,68},{5,69},{6,70},{7,71},{8,72},{9,... | collective-permute-start | bytes 3538952 | tf_op jit(solution)/shard_map/ppermute | solution.py:62
  112.4 11.0 %collective-permute-start.35 = (bf16[8,48,1536]{2,1,0:T(8,128)(2,1)}, bf16[8,48,1536]{2,1,0:T(8,128)(2,1)}, u32[]{:S(2)}, u32[]{:S(2)}) collective-permute-start(bf16[8,48,1536]{2,1,0:T(8,128)(2,1)} %copy-done.5), channel_id=1, source_target_pairs={{0,64},{1,65},{2,66},{3,67},{4,68},{5,69},{6,70},{7,71},{8,72},{9,... | collective-permute-start | bytes 3538952 | tf_op jit(solution)/shard_map/ppermute | solution.py:62
  156.5 25.1 %collective-permute-start.42 = (bf16[2,14,8,1536]{3,2,1,0:T(8,128)(2,1)S(1)}, bf16[2,14,8,1536]{3,2,1,0:T(8,128)(2,1)S(1)}, u32[]{:S(2)}, u32[]{:S(2)}) collective-permute-start(bf16[2,14,8,1536]{3,2,1,0:T(8,128)(2,1)S(1)} %get-tuple-element.10), channel_id=1, source_target_pairs={{0,1},{1,2},{2,3},{3,4},{4,5},{5,6},{6,7},{7,8},{8,9},{9,10},{10,1... | collective-permute-start | bytes 2064392 | tf_op jit(solution)/shard_map/ppermute | solution.py:67
  157.6 24.1 %collective-permute-start.40 = (bf16[2,2,8,1536]{3,2,1,0:T(8,128)(2,1)S(1)}, bf16[2,2,8,1536]{3,2,1,0:T(8,128)(2,1)S(1)}, u32[]{:S(2)}, u32[]{:S(2)}) collective-permute-start(bf16[2,2,8,1536]{3,2,1,0:T(8,128)(2,1)S(1)} %get-tuple-element.8), channel_id=1, source_target_pairs={{0,65},{1,66},{2,67},{3,68},{4,69},{5,70},{6,71},{7,72},{8,73},{9,... | collective-permute-start | bytes 294920 | tf_op jit(solution)/shard_map/ppermute | solution.py:62
  162.8 18.8 %collective-permute-start.41 = (bf16[2,2,8,1536]{3,2,1,0:T(8,128)(2,1)S(1)}, bf16[2,2,8,1536]{3,2,1,0:T(8,128)(2,1)S(1)}, u32[]{:S(2)}, u32[]{:S(2)}) collective-permute-start(bf16[2,2,8,1536]{3,2,1,0:T(8,128)(2,1)S(1)} %get-tuple-element.9), channel_id=1, source_target_pairs={{0,64},{64,128},{128,192},{1,65},{65,129},{129,193},{2,66},{66,130... | collective-permute-start | bytes 294920 | tf_op jit(solution)/shard_map/ppermute | solution.py:72
  (33 other events, 443.4 us)
